TPU v7x, 128 devices: a whole 4x4x4 slice. The times are simulated.
128 devices in a mesh: ctx: 32 (over y, x, core), head: 4 (over z).
Axes of the slice: x: 4, y: 4, z: 4, core: 2. Of those that a mesh axis runs over, the one named last changes fastest.
Arguments:
- queries: bfloat16 [192, 8192], P('ctx', 'head'), may hold values from -14 to 14
- keys: bfloat16 [262144, 1024], P('ctx', 'head'), may hold values from -8 to 8
- values: bfloat16 [262144, 1024], P('ctx', 'head'), may hold values from -6 to 6
- lengths: int32 [32], P('ctx'), may hold values from 1 to 8192, as said below
Outputs:
- mixed: bfloat16 [192, 8192], P('ctx')
- log_norm: float32 [192, 64], P('ctx')
Inputs may be any that keep to these rules, and one draw needn't show every extreme that they name: `lengths`: block 0 is always full; the last block holds at most 4096 valid tokens; every other block at least 4096.
All inputs are finite; a program needn't handle non-finite values.
Results may differ from a plain program's by a relative error of at most 0.0033.
Values may be sent and summed in bfloat16 or wider, within the bound.
No kernel may reach another device: no remote copies, remote signals or barrier semaphores. Data moves between devices by JAX's collectives and lax.ppermute only.
A program may use at most 256 MiB of HBM per device.

v0:
```python
import math

import jax
import jax.numpy as jnp
from jax import lax
from jax.sharding import PartitionSpec as P

DH = 128
BLOCK = 8192
TILE = 1024


masked_score = -1e30


def on_device(queries, keys, values, lengths):
    gathered = lax.all_gather(queries, "ctx", axis=0, tiled=True)
    rows_all = gathered.shape[0]
    kv_local = keys.shape[1] // DH
    group_size = gathered.shape[1] // DH // kv_local
    query_heads = gathered.reshape(rows_all, kv_local, group_size, DH)
    score_scale = 1.0 / math.sqrt(DH)
    per_block = BLOCK // TILE
    tile_count = keys.shape[0] // TILE
    key_tiles = keys.reshape(tile_count, TILE, kv_local, DH)
    value_tiles = values.reshape(tile_count, TILE, kv_local, DH)
    tile_limit = (
        jnp.repeat(lengths, per_block, total_repeat_length=tile_count)
        - jnp.arange(tile_count, dtype=jnp.int32) % per_block * TILE
    )

    def one_tile(state_carry, inputs):
        key_tile, value_tile, limit = inputs
        scores = (
            jnp.einsum("qkgd,ckd->kgqc", query_heads, key_tile, preferred_element_type=jnp.float32)
            * score_scale
        )
        is_valid = jnp.arange(TILE, dtype=jnp.int32) < limit
        scores = jnp.where(is_valid, scores, masked_score)
        tile_peak = jnp.max(scores, axis=-1)
        weights = jnp.exp(scores - tile_peak[..., None])
        tile_total = jnp.sum(weights, axis=-1)
        tile_probs = weights.astype(jnp.bfloat16)
        tile_out = jnp.einsum(
            "kgqc,ckd->qkgd", tile_probs, value_tile, preferred_element_type=jnp.float32
        )
        return (state_carry, (tile_peak, tile_total, tile_out))

    unused, stacked = lax.scan(one_tile, jnp.int32(0), (key_tiles, value_tiles, tile_limit))
    peaks = jnp.transpose(stacked[0], (0, 3, 1, 2))
    totals = jnp.transpose(stacked[1], (0, 3, 1, 2))
    outputs = stacked[2]
    local_peak = jnp.max(peaks, axis=0)
    own_rows = rows_all // lax.axis_size("ctx")
    first_row = lax.axis_index("ctx") * own_rows
    global_peak = lax.pmax(local_peak, "ctx")
    scaled = jnp.exp(peaks - global_peak[None])
    numerator = jnp.sum(scaled[..., None] * outputs, axis=0)
    denominator = jnp.sum(scaled * totals, axis=0)
    numerator, denominator = (numerator.reshape(rows_all, -1), denominator.reshape(rows_all, -1))
    numer_own, denom_own = (
        lax.psum_scatter(numerator, "ctx", scatter_dimension=0, tiled=True),
        lax.psum_scatter(denominator, "ctx", scatter_dimension=0, tiled=True),
    )
    peak_own = lax.dynamic_slice_in_dim(global_peak.reshape(rows_all, -1), first_row, own_rows, 0)
    numer_all, denom_all, peak_all = (
        lax.all_gather(numer_own, "head", axis=1, tiled=True),
        lax.all_gather(denom_own, "head", axis=1, tiled=True),
        lax.all_gather(peak_own, "head", axis=1, tiled=True),
    )
    head_total = denom_all.shape[1]
    mixed = (
        (numer_all.reshape(own_rows, head_total, DH) / denom_all[..., None])
        .reshape(own_rows, head_total * DH)
        .astype(jnp.bfloat16)
    )
    log_norm = peak_all + jnp.log(denom_all)
    return (mixed, log_norm)


def solution(mesh):
    return jax.shard_map(
        on_device,
        mesh=mesh,
        in_specs=(P("ctx", "head"), P("ctx", "head"), P("ctx", "head"), P("ctx")),
        out_specs=(P("ctx", None), P("ctx", None)),
        check_vma=False,
    )
```

profile of v0, /device:TPU:0, one launch (start us, length us, event | category | flops | bytes accessed | tf_op | source)
XLA Modules:
  0.0 533.1 jit_solution(8696095357065948002)
XLA Ops:
  0.7 6.9 %reshape.109 = bf16[8,1024,2,128]{3,2,1,0:T(2,128)(2,1)} reshape(bf16[8192,256]{1,0:T(8,128)(2,1)} %param.11) | data formatting | bytes 8388608 | tf_op jit(solution)/shard_map/reshape | solution.py:25
  7.6 6.9 %reshape.110 = bf16[8,1024,2,128]{3,2,1,0:T(2,128)(2,1)} reshape(bf16[8192,256]{1,0:T(8,128)(2,1)} %param.12) | data formatting | bytes 8388608 | tf_op jit(solution)/shard_map/reshape | solution.py:26
  14.5 25.3 %all-gather = bf16[32,6,2048]{2,1,0:T(8,128)(2,1)S(1)} all-gather(bf16[1,6,2048]{2,1,0:T(8,128)(2,1)S(1)} %bitcast.104), channel_id=1, replica_groups=mesh['ctx'=32,'head'=4] {'ctx'}, dimensions={0}, use_global_device_ids=true | all-gather | bytes 811008 | tf_op jit(solution)/shard_map/all_gather | solution.py:17
  41.6 104.7 %while.16 = (s32[]{:T(128)}, f32[8,2,8,192]{3,2,1,0:T(8,128)S(1)}, f32[8,2,8,192]{3,2,1,0:T(8,128)S(1)}, f32[8,192,2,8,128]{4,1,3,2,0:T(8,128)}, s32[8]{0:T(128)...) while((s32[]{:T(128)}, f32[8,2,8,192]{3,2,1,0:T(8,128)S(1)}, ...), condition=%wide.region_3.4_spmd, body=%wide.region_0.3_spmd.sunk | while | flops 1645210624 | bytes 43373176 | solution.py:49
  42.9 1.4 constant_dynamic-slice_fusion.6
  44.3 2.0 bitcast_reduce_fusion.3
  46.2 1.4 constant_dynamic-slice_fusion.7
  47.7 3.9 bitcast_dynamic-update-slice_fusion.6
  51.5 3.1 fusion.25
  55.9 1.4 constant_dynamic-slice_fusion.6
  57.3 2.0 bitcast_reduce_fusion.3
  59.3 1.4 constant_dynamic-slice_fusion.7
  60.7 3.9 bitcast_dynamic-update-slice_fusion.6
  64.6 3.1 fusion.25
  69.0 1.4 constant_dynamic-slice_fusion.6
  70.4 2.0 bitcast_reduce_fusion.3
  72.4 1.4 constant_dynamic-slice_fusion.7
  73.8 3.8 bitcast_dynamic-update-slice_fusion.6
  77.7 3.1 fusion.25
  82.1 1.4 constant_dynamic-slice_fusion.6
  83.5 2.0 bitcast_reduce_fusion.3
  85.5 1.4 constant_dynamic-slice_fusion.7
  86.9 3.9 bitcast_dynamic-update-slice_fusion.6
  90.8 3.1 fusion.25
  95.2 1.4 constant_dynamic-slice_fusion.6
  96.6 2.0 bitcast_reduce_fusion.3
  100.0 3.8 bitcast_dynamic-update-slice_fusion.6
  103.8 3.1 fusion.25
  108.2 1.4 constant_dynamic-slice_fusion.6
  109.6 2.0 bitcast_reduce_fusion.3
  113.0 3.9 bitcast_dynamic-update-slice_fusion.6
  117.0 3.1 fusion.25
  121.4 1.4 constant_dynamic-slice_fusion.6
  122.8 2.0 bitcast_reduce_fusion.3
  126.2 3.9 bitcast_dynamic-update-slice_fusion.6
  130.1 3.1 fusion.25
  134.5 1.4 constant_dynamic-slice_fusion.6
  135.9 2.0 bitcast_reduce_fusion.3
  137.9 1.4 constant_dynamic-slice_fusion.7
  139.3 3.9 bitcast_dynamic-update-slice_fusion.6
  143.1 3.1 fusion.25
  146.3 126.4 %pmax.7 = f32[192,2,8]{0,2,1:T(8,128)S(1)} all-reduce(f32[192,2,8]{0,2,1:T(8,128)S(1)} %bitcast_reduce_fusion.1), channel_id=1, replica_groups=mesh['ctx'=32,'head'=4] {'ctx'}, use_global_device_ids=true, to_apply=%region_5.6 | all-reduce | flops 3072 | bytes 24576 | tf_op jit(solution)/shard_map/pmax | solution.py:56
  272.7 7.8 %multiply_reduce_fusion = f32[192,2,8,128]{3,0,2,1:T(8,128)S(1)} fusion(f32[8,192,2,8,128]{4,1,3,2,0:T(8,128)} %get-tuple-element.71, f32[8,192,2,8]{1,3,2,0:T(8,128)S(1)} %get-tuple-element.114), kind=kLoop, calls=%fused_computation.19 | loop fusion | flops 5898240 | bytes 14254080 | tf_op jit(solution)/shard_map/reduce_sum | solution.py:58
  282.0 73.9 %fusion = f32[8,2048]{1,0:T(8,128)S(1)} fusion(f32[192,2048]{1,0:T(8,128)S(1)} %bitcast.100), kind=kCustom, calls=%all-reduce-scatter | all-reduce-scatter fusion | flops 524289 | bytes 1638912
  362.5 123.8 %all-reduce.1 = f32[192,16]{0,1:T(8,128)S(1)} all-reduce(f32[192,16]{0,1:T(8,128)S(1)} %bitcast.102), channel_id=3, replica_groups=mesh['ctx'=32,'head'=4] {'ctx'}, use_global_device_ids=true, to_apply=%region_9.10.clone | all-reduce | flops 3072 | bytes 24576
  487.6 13.1 %all-gather.1 = f32[4,16,6]{1,2,0:T(8,128)S(1)} all-gather(f32[1,16,6]{1,2,0:T(8,128)S(1)} %bitcast.105), channel_id=1, replica_groups=mesh['ctx'=32,'head'=4] {'head'}, dimensions={0}, use_global_device_ids=true | all-gather | bytes 1920 | tf_op jit(solution)/shard_map/all_gather | solution.py:68
  501.1 11.9 %all-gather.2 = f32[4,16,6]{1,2,0:T(8,128)S(1)} all-gather(f32[1,16,6]{1,2,0:T(8,128)S(1)} %bitcast.106), channel_id=1, replica_groups=mesh['ctx'=32,'head'=4] {'head'}, dimensions={0}, use_global_device_ids=true | all-gather | bytes 1920 | tf_op jit(solution)/shard_map/all_gather | solution.py:69
  520.0 12.3 %all_gather.13 = f32[6,8192]{1,0:T(8,128)S(1)} all-gather(f32[6,2048]{1,0:T(8,128)S(1)} %constant_dynamic-slice_fusion.2), channel_id=1, replica_groups=mesh['ctx'=32,'head'=4] {'head'}, dimensions={1}, use_global_device_ids=true | all-gather | bytes 245760 | tf_op jit(solution)/shard_map/all_gather | solution.py:67
  (72 shorter events, 31.5 us)
Async XLA Ops:
  0.6 13.9 %copy-start = (bf16[6,2048]{1,0:T(8,128)(2,1)S(1)}, bf16[6,2048]{1,0:T(8,128)(2,1)}, u32[]{:S(2)}) copy-start(bf16[6,2048]{1,0:T(8,128)(2,1)} %param.10) | copy-start | bytes 73732
  146.3 340.0 %copy-start.1 = (u32[128]{0:T(128)S(1)}, u32[128]{0:T(128)}, u32[]{:S(2)}) copy-start(u32[128]{0:T(128)} %constant.150) | copy-start | bytes 1540
  355.9 158.5 %collective-permute-start = (f32[8,2048]{1,0:T(8,128)S(1)}, f32[8,2048]{1,0:T(8,128)S(1)}, u32[]{:S(2)}, u32[]{:S(2)}) collective-permute-start(f32[8,2048]{1,0:T(8,128)S(1)} %fusion), channel_id=1, source_target_pairs={{0,4},{4,8},{8,12},{12,16},{16,20},{20,24},{24,28},{28,32},{32,36}... | collective-permute-start | bytes 196616
  357.2 158.5 %collective-permute-start.1 = (f32[8,2048]{1,0:T(8,128)S(1)}, f32[8,2048]{1,0:T(8,128)S(1)}, u32[]{:S(2)}, u32[]{:S(2)}) collective-permute-start(f32[8,2048]{1,0:T(8,128)S(1)} %fusion), channel_id=1, source_target_pairs={{0,8},{4,12},{8,16},{12,20},{16,24},{20,28},{24,32},{28,36},{32,40... | collective-permute-start | bytes 196616
  358.5 159.8 %collective-permute-start.2 = (f32[8,2048]{1,0:T(8,128)S(1)}, f32[8,2048]{1,0:T(8,128)S(1)}, u32[]{:S(2)}, u32[]{:S(2)}) collective-permute-start(f32[8,2048]{1,0:T(8,128)S(1)} %fusion), channel_id=1, source_target_pairs={{0,12},{4,16},{8,20},{12,24},{16,28},{20,32},{24,36},{28,40},{32,4... | collective-permute-start | bytes 196616
  359.8 158.5 %collective-permute-start.3 = (f32[8,2048]{1,0:T(8,128)S(1)}, f32[8,2048]{1,0:T(8,128)S(1)}, u32[]{:S(2)}, u32[]{:S(2)}) collective-permute-start(f32[8,2048]{1,0:T(8,128)S(1)} %fusion), channel_id=1, source_target_pairs={{0,16},{4,20},{8,24},{12,28},{16,32},{20,36},{24,40},{28,44},{32,4... | collective-permute-start | bytes 196616
  361.1 152.0 %collective-permute-start.7 = (f32[6,2048]{1,0:T(8,128)S(1)}, f32[6,2048]{1,0:T(8,128)S(1)}, u32[]{:S(2)}, u32[]{:S(2)}) collective-permute-start(f32[6,2048]{1,0:T(8,128)S(1)} %slice.18), channel_id=1, source_target_pairs={{0,32},{4,36},{8,40},{12,44},{16,48},{20,52},{24,56},{28,60},{32,6... | collective-permute-start | bytes 147464
  513.1 5.2 collective-permute-start.4
  514.4 3.9 collective-permute-start.5
  515.8 3.2 collective-permute-start.6
where the time goes:
time: 535 us; the launch traced here: 533 us
  blocking collectives  387 us (72%)
  matrix products  46.8 us (9%)
  local copies, waits for them, and re-layouts  46.1 us (9%)
  other arithmetic  39.4 us (7%)
  starting transfers between devices  10.3 us (2%)
    unnamed x2, blocking collectives  198 us
    pmax x1, blocking collectives, on_device(): global_peak = lax.pmax(local_peak, 'ctx')  126 us
    dot_general x8, matrix products, one_tile(): jnp.einsum('kgqc,ckd->qkgd', tile_probs, value_tile, preferred_element_ty...  31 us
    dynamic_slice x24, local copies, waits for them, and re-layouts, on_device(): lax.scan(one_tile, jnp.int32(0), (key_tiles, value_tiles, tile_limit))  27.2 us
    all_gather x1, blocking collectives, on_device(): gathered = lax.all_gather(queries, 'ctx', axis=0, tiled=True)  25.3 us
    reduce_sum x8, other arithmetic, one_tile(): tile_total = jnp.sum(weights, axis=-1)  25 us
    dot_general x8, matrix products, one_tile(): jnp.einsum('qkgd,ckd->kgqc', query_heads, key_tile, preferred_element_typ...  15.8 us
    all_gather x1, blocking collectives, on_device(): lax.all_gather(denom_own, 'head', axis=1, tiled=True)  13.1 us
  transfers between devices with their start and end apart: 8, of which 1 were waited for; matrix products, arithmetic and copies ran while one was open for 0% of the time, Pallas kernels for 0%

commit v1 on v0

v1 whole, which is shorter than its diff:
```python
import math

import jax
import jax.numpy as jnp
from jax import lax
from jax.experimental import pallas as pl
from jax.experimental.pallas import tpu as pltpu
from jax.sharding import PartitionSpec as P

DH = 128
f32, bf16 = jnp.float32, jnp.bfloat16
LOG2E = 1.4426950408889634
LN2 = 0.6931471805599453
TO_LOG2 = LOG2E / math.sqrt(DH)

CHIPS, CORES = 16, 2
TOK, GRP, KV = 6, 8, 2
ROWS = TOK * GRP
HALF = CHIPS * ROWS
COLS = CORES * HALF
CTX = 8192
CHUNK = 2048
PROBE = 256
LROW, MROW, AUG = DH, DH + 8, DH + 16
MSG = KV * ROWS + 8

VMEM = pl.BlockSpec(memory_space=pltpu.VMEM)
SMEM = pl.BlockSpec(memory_space=pltpu.SMEM)
ANY = pl.BlockSpec(memory_space=pl.ANY)
PARAMS = pltpu.CompilerParams(vmem_limit_bytes=60 * 2**20)


def spread_body(q_ref, out_ref):
    q = q_ref[...].astype(f32)
    rows = jnp.concatenate([q[:, i * DH : (i + 1) * DH] for i in range(KV * GRP)], axis=0)
    out_ref[...] = jnp.broadcast_to(rows.astype(bf16)[None], out_ref.shape)


def attend_body(
    len_ref, q_own, q_other, k_hbm, v_hbm, own_ref, other_ref, kbuf, vbuf, qt, vt, peak, ksem, vsem
):
    chunks = CTX // CHUNK
    outs = (own_ref, other_ref)

    def k_copy(c):
        part = pl.ds(c * CHUNK, CHUNK)
        return pltpu.make_async_copy(k_hbm.at[part], kbuf.at[part], ksem.at[c])

    def v_copy(c):
        part = pl.ds(c * CHUNK, CHUNK)
        return pltpu.make_async_copy(v_hbm.at[part], vbuf.at[part], vsem.at[c])

    for c in range(chunks):
        k_copy(c).start()
        v_copy(c).start()
    valid = len_ref[0]
    for h in range(KV):
        for i, src in enumerate((q_own, q_other)):
            x = src[:, h * ROWS : (h + 1) * ROWS, :].reshape(HALF, DH)
            qt[h, :, i * HALF : (i + 1) * HALF] = x.astype(f32).T.astype(bf16)
    k_copy(0).wait()
    v_copy(0).wait()

    for h in range(KV):
        s = jnp.dot(kbuf[0:PROBE, h * DH : (h + 1) * DH], qt[h], preferred_element_type=f32)
        pos = lax.broadcasted_iota(jnp.int32, (PROBE, 1), 0)
        s = jnp.where(pos < valid, s, -1e30)
        peak[h] = jnp.max(s, axis=0, keepdims=True) * TO_LOG2

    def turn_values(h, first, size):
        ok = lax.broadcasted_iota(jnp.int32, (1, size), 1) + first < valid
        v = vbuf[pl.ds(first, size), h * DH : (h + 1) * DH].astype(f32).T
        vt[0:DH, 0:size] = jnp.where(ok, v, 0.0).astype(bf16)
        ones = jnp.broadcast_to(jnp.where(ok, 1.0, 0.0), (AUG - DH, size))
        vt[DH:AUG, 0:size] = ones.astype(bf16)

    def chunk(c, h, fresh):
        first = pl.multiple_of(c * CHUNK, CHUNK)
        turn_values(h, first, CHUNK)
        k = kbuf[pl.ds(first, CHUNK), h * DH : (h + 1) * DH]
        for i, out in enumerate(outs):
            part = slice(i * HALF, (i + 1) * HALF)
            s = jnp.dot(k, qt[h, :, part], preferred_element_type=f32)
            p = jnp.exp2(jnp.minimum(s * TO_LOG2 - peak[h, :, part], 100.0)).astype(bf16)
            pv = jnp.dot(vt[...], p, preferred_element_type=f32)
            if fresh:
                out[h] = pv
            else:
                out[h] += pv

    for h in range(KV):
        chunk(0, h, True)

    def later(c, carry):
        k_copy(c).wait()
        v_copy(c).wait()

        @pl.when(c * CHUNK < valid)
        def _():
            for h in range(KV):
                chunk(c, h, False)

        return carry

    lax.fori_loop(1, chunks, later, 0)

    low = jnp.minimum(jnp.min(own_ref[:, LROW, :]), jnp.min(other_ref[:, LROW, :]))
    high = jnp.maximum(jnp.max(own_ref[:, LROW, :]), jnp.max(other_ref[:, LROW, :]))

    @pl.when(jnp.logical_not((low > 0.25) & (high < 2.0**60)))
    def _():
        size = 512

        def part_scores(h, i, first):
            k = kbuf[pl.ds(first, size), h * DH : (h + 1) * DH]
            s = jnp.dot(k, qt[h, :, i * HALF : (i + 1) * HALF], preferred_element_type=f32)
            pos = lax.broadcasted_iota(jnp.int32, (size, 1), 0) + first
            return jnp.where(pos < valid, s * TO_LOG2, -1e30)

        for h in range(KV):
            for i, out in enumerate(outs):
                part = slice(i * HALF, (i + 1) * HALF)

                def top(c, best):
                    s = part_scores(h, i, pl.multiple_of(c * size, size))
                    return jnp.maximum(best, jnp.max(s, axis=0, keepdims=True))

                peak[h, :, part] = lax.fori_loop(
                    0, CTX // size, top, jnp.full((1, HALF), -1e30, f32)
                )
                out[h] = jnp.zeros((AUG, HALF), f32)

                def add(c, carry):
                    first = pl.multiple_of(c * size, size)
                    turn_values(h, first, size)
                    p = jnp.exp2(part_scores(h, i, first) - peak[h, :, part]).astype(bf16)
                    out[h] += jnp.dot(vt[:, 0:size], p, preferred_element_type=f32)
                    return carry

                lax.fori_loop(0, CTX // size, add, 0)

    for h in range(KV):
        for i, out in enumerate(outs):
            part = slice(i * HALF, (i + 1) * HALF)
            out[h, MROW:AUG, :] = jnp.broadcast_to(peak[h, :, part], (AUG - MROW, HALF))


def pair_body(a_ref, b_ref, out_ref):
    for h in range(KV):
        ma, mb = a_ref[h, MROW : MROW + 1, :], b_ref[h, MROW : MROW + 1, :]
        top = jnp.maximum(ma, mb)
        wa, wb = jnp.exp2(ma - top), jnp.exp2(mb - top)
        total = wa * a_ref[h, LROW : LROW + 1, :] + wb * b_ref[h, LROW : LROW + 1, :]
        num = a_ref[h, 0:DH, :] * (wa / total) + b_ref[h, 0:DH, :] * (wb / total)
        out_ref[:, h * ROWS : (h + 1) * ROWS, :] = num.T.reshape(CHIPS, ROWS, DH)
        norm = top + jnp.log2(total)
        for c in range(CHIPS):
            out_ref[c, KV * ROWS : KV * ROWS + 1, h * ROWS : (h + 1) * ROWS] = norm[
                :, c * ROWS : (c + 1) * ROWS
            ]


def merge_body(in_ref, out_ref):
    rows = KV * ROWS
    norm = in_ref[:, rows, :]
    norm = jnp.where(lax.broadcasted_iota(jnp.int32, norm.shape, 1) < rows, norm, 0.0)
    top = jnp.max(norm, axis=0, keepdims=True)
    w = jnp.exp2(norm - top)
    total = jnp.sum(w, axis=0, keepdims=True)
    w = (w / total).T
    o = in_ref[0, 0:rows, :] * w[0:rows, 0:1]
    for c in range(1, CHIPS):
        o = o + in_ref[c, 0:rows, :] * w[0:rows, c : c + 1]
    out_ref[:, 0:rows, :] = jnp.broadcast_to(o[None], (out_ref.shape[0], rows, DH))
    norm = (top + jnp.log2(total)) * LN2
    out_ref[:, rows:MSG, :] = jnp.broadcast_to(norm[None], (out_ref.shape[0], MSG - rows, DH))


def finish_body(in_ref, mixed_ref, norm_ref):
    rows, heads = KV * ROWS, KV * GRP
    parts = in_ref.shape[0]
    token = lax.broadcasted_iota(jnp.int32, (8, DH), 0)
    lane = lax.broadcasted_iota(jnp.int32, (8, DH), 1)
    lane_of = lax.broadcasted_iota(jnp.int32, (DH, parts * heads), 0)
    head_of = lax.broadcasted_iota(jnp.int32, (DH, parts * heads), 1)
    norm = jnp.zeros((8, parts * heads), f32)
    for z in range(parts):
        o = in_ref[z, 0:rows, :].astype(bf16).astype(f32)
        for i in range(heads):
            mixed_ref[:, (z * heads + i) * DH : (z * heads + i + 1) * DH] = o[
                i * TOK : (i + 1) * TOK, :
            ].astype(bf16)
        mine = jnp.where((lane % TOK == token) & (lane < rows), in_ref[z, rows : rows + 1, :], 0.0)
        pick = jnp.where(lane_of // TOK + z * heads == head_of, 1.0, 0.0)
        pick = jnp.where(lane_of < rows, pick, 0.0)
        norm = norm + jnp.dot(
            mine, pick, preferred_element_type=f32, precision=lax.Precision.HIGHEST
        )
    norm_ref[...] = norm[0:TOK, :]


def call(body, out_shape, in_specs, scratch=()):
    many = isinstance(out_shape, tuple)
    return pl.pallas_call(
        body,
        out_shape=out_shape,
        in_specs=in_specs,
        out_specs=(VMEM,) * len(out_shape) if many else VMEM,
        scratch_shapes=list(scratch),
        compiler_params=PARAMS,
    )


def on_device(queries, keys, values, lengths):
    shape = jax.ShapeDtypeStruct
    same_core = [[2 * i + c for i in range(CHIPS)] for c in range(CORES)]
    swap = [(i, i ^ 1) for i in range(CHIPS * CORES)]
    parts = lax.axis_size("head")

    sent = call(spread_body, shape((CHIPS, KV * ROWS, DH), bf16), [VMEM])(queries)
    q_own = lax.all_to_all(sent, "ctx", 0, 0, tiled=True, axis_index_groups=same_core)
    q_other = lax.ppermute(q_own, "ctx", swap)
    acc = shape((KV, AUG, HALF), f32)
    own, other = call(
        attend_body,
        (acc, acc),
        [SMEM, VMEM, VMEM, ANY, ANY],
        [
            pltpu.VMEM((CTX, KV * DH), bf16),
            pltpu.VMEM((CTX, KV * DH), bf16),
            pltpu.VMEM((KV, DH, COLS), bf16),
            pltpu.VMEM((AUG, CHUNK), bf16),
            pltpu.VMEM((KV, 1, COLS), f32),
            pltpu.SemaphoreType.DMA((CTX // CHUNK,)),
            pltpu.SemaphoreType.DMA((CTX // CHUNK,)),
        ],
    )(lengths, q_own, q_other, keys, values)
    partner = lax.ppermute(other, "ctx", swap)
    sent = call(pair_body, shape((CHIPS, MSG, DH), f32), [VMEM, VMEM])(own, partner)
    got = lax.all_to_all(sent, "ctx", 0, 0, tiled=True, axis_index_groups=same_core)
    sent = call(merge_body, shape((parts, MSG, DH), f32), [VMEM])(got)
    got = lax.all_to_all(sent, "head", 0, 0, tiled=True)
    heads = parts * KV * GRP
    return call(finish_body, (shape((TOK, heads * DH), bf16), shape((TOK, heads), f32)), [VMEM])(
        got
    )


def solution(mesh):
    return jax.shard_map(
        on_device,
        mesh=mesh,
        in_specs=(P("ctx", "head"), P("ctx", "head"), P("ctx", "head"), P("ctx")),
        out_specs=(P("ctx", None), P("ctx", None)),
        check_vma=False,
    )
```

time: 535 us -> 94.7 us (0.18)
  blocking collectives: 387 us -> 49 us
  matrix products: 46.8 us -> 0 us
  local copies, waits for them, and re-layouts: 46.1 us -> 1.7 us
  other arithmetic: 39.4 us -> 0 us
  Pallas kernels: 0 us -> 38.4 us
  starting transfers between devices: 10.3 us -> 0.09 us
    unnamed x2 -> x0, blocking collectives: 198 us -> none
    pmax x1 -> x0, blocking collectives: 126 us -> none  [on_device(): global_peak = lax.pmax(local_peak, 'ctx')]
    all_gather x4 -> x0, blocking collectives: 62.6 us -> none  [the longest x1 25.3 us: on_device(): gathered = lax.all_gather(queries, 'ctx', axis=0, tiled=True)]
    all_to_all x0 -> x3, blocking collectives: none -> 49 us  [the longest x2 37.1 us: on_device(): lax.all_to_all(sent, 'ctx', 0, 0, tiled=True, axis_index_groups=same_core)]
    dot_general x16 -> x0, matrix products: 46.8 us -> none  [the longest x8 31 us: one_tile(): jnp.einsum('kgqc,ckd->qkgd', tile_probs, value_tile, preferred_element_ty...]
    pallas_call x0 -> x5, Pallas kernels: none -> 38.4 us  [the longest x1 30.1 us: on_device(): call(attend_body, (acc, acc), [SMEM, VMEM, VMEM, ANY, ANY], [pltpu.VMEM((...]
    reduce_sum x10 -> x0, other arithmetic: 32.8 us -> none  [the longest x8 25 us: one_tile(): tile_total = jnp.sum(weights, axis=-1)]
    dynamic_slice x24 -> x0, local copies, waits for them, and re-layouts: 27.2 us -> none  [on_device(): lax.scan(one_tile, jnp.int32(0), (key_tiles, value_tiles, tile_limit))]
  transfers between devices with their start and end apart: 8 -> 2, of which waited for: 1 -> 2; matrix products, arithmetic and copies ran while one was open for 0% -> 0% of each run, Pallas kernels for 0% -> 0%
where the time goes in v1:
time: 94.7 us; the launch traced here: 94.1 us
  blocking collectives  49 us (52%)
  Pallas kernels  38.4 us (41%)
  waiting for transfers between devices  3.69 us (4%)
  local copies, waits for them, and re-layouts  1.7 us (2%)
  between operations  1.31 us (1%)
    all_to_all x2, blocking collectives, on_device(): lax.all_to_all(sent, 'ctx', 0, 0, tiled=True, axis_index_groups=same_core)  37.1 us
    pallas_call x1, Pallas kernels, on_device(): call(attend_body, (acc, acc), [SMEM, VMEM, VMEM, ANY, ANY], [pltpu.VMEM((...  30.1 us
    all_to_all x1, blocking collectives, on_device(): got = lax.all_to_all(sent, 'head', 0, 0, tiled=True)  11.8 us
    pallas_call x1, Pallas kernels, on_device(): call(pair_body, shape((CHIPS, MSG, DH), f32), [VMEM, VMEM])(own, partner)  2.7 us
    ppermute x1, waiting for transfers between devices, on_device(): partner = lax.ppermute(other, 'ctx', swap)  2.62 us
    pallas_call x1, Pallas kernels, on_device(): sent = call(merge_body, shape((parts, MSG, DH), f32), [VMEM])(got)  2.28 us
  transfers between devices with their start and end apart: 2, of which 2 were waited for; matrix products, arithmetic and copies ran while one was open for 0% of the time, Pallas kernels for 0%

profile of v1, /device:TPU:0, one launch (start us, length us, event | category | flops | bytes accessed | tf_op | source)
XLA Modules:
  0.0 94.1 jit_solution(12921055513766010687)
XLA Ops:
  0.6 1.5 %shard_map.59 = bf16[16,96,128]{2,1,0:T(8,128)(2,1)} custom-call(bf16[6,2048]{1,0:T(8,128)(2,1)} %q_ref.1), custom_call_target="tpu_custom_call" | custom-call | tf_op jit(solution)/shard_map/pallas_call | solution.py:220
  2.2 17.2 %all_to_all.15.q_own = bf16[16,96,128]{2,1,0:T(8,128)(2,1)S(1)} all-to-all(bf16[16,96,128]{2,1,0:T(8,128)(2,1)} %shard_map.59), channel_id=1, replica_groups={{0,8,16,24,32,40,48,56,64,72,80,88,96,104,112,120},{4,12,20,28,36,44,52..., dimensions={0} | all-to-all | bytes 786432 | tf_op jit(solution)/shard_map/all_to_all | solution.py:221
  19.4 0.0 copy-start
  19.4 0.0 collective-permute-start
  20.0 1.1 %collective-permute-done.q_other = bf16[16,96,128]{2,1,0:T(8,128)(2,1)S(1)} collective-permute-done((bf16[16,96,128]{2,1,0:T(8,128)(2,1)S(1)}, bf16[16,96,128]{2,1,0:T(8,128)(2,1)S(1)}, u32[]{:S(2)}, u32[]{:S(2)}) %collective-permute-start) | collective-permute-done | bytes 393248 | tf_op jit(solution)/shard_map/ppermute | solution.py:222
  21.1 0.0 copy-done
  21.1 0.0 copy-start.2
  21.1 0.7 copy-done.2
  21.8 30.1 %shard_map.60 = (f32[2,144,768]{2,1,0:T(8,128)}, f32[2,144,768]{2,1,0:T(8,128)}) custom-call(s32[1]{0:T(128)S(6)} %copy.6.len_ref, bf16[16,96,128]{2,1,0:T(8,128)(2,1)} %copy-done, bf16[16,96,128]{2,1,0:T(8,128)(2,1)} %copy-done.2, bf16[8192,256]{1,0:T(8,128)(2,1)} %k_hbm.1, bf16[8192,256]{1,0:T(8,128)(2,1)} %v_hbm.1), custom_call_target="tpu_custom_call" | custom-call | tf_op jit(solution)/shard_map/pallas_call | solution.py:224
  51.9 0.1 collective-permute-start.1
  52.0 2.6 %collective-permute-done.1.b_ref = f32[2,144,768]{2,1,0:T(8,128)S(1)} collective-permute-done((f32[2,144,768]{2,1,0:T(8,128)}, f32[2,144,768]{2,1,0:T(8,128)S(1)}, u32[]{:S(2)}, u32[]{:S(2)}) %collective-permute-start.1) | collective-permute-done | bytes 884768 | tf_op jit(solution)/shard_map/ppermute | solution.py:238
  54.6 0.0 copy-start.1
  54.6 0.9 %copy-done.1 = f32[2,144,768]{2,1,0:T(8,128)} copy-done((f32[2,144,768]{2,1,0:T(8,128)}, f32[2,144,768]{2,1,0:T(8,128)S(1)}, u32[]{:S(2)}) %copy-start.1) | copy-done | bytes 884760
  55.6 2.7 %shard_map.61 = f32[16,104,128]{2,1,0:T(8,128)} custom-call(f32[2,144,768]{2,1,0:T(8,128)} %get-tuple-element.4.a_ref, f32[2,144,768]{2,1,0:T(8,128)} %copy-done.1), custom_call_target="tpu_custom_call" | custom-call | tf_op jit(solution)/shard_map/pallas_call | solution.py:239
  58.3 19.9 %all_to_all.16.in_ref = f32[16,104,128]{2,1,0:T(8,128)} all-to-all(f32[16,104,128]{2,1,0:T(8,128)} %shard_map.61), channel_id=1, replica_groups={{0,8,16,24,32,40,48,56,64,72,80,88,96,104,112,120},{4,12,20,28,36,44,52..., dimensions={0} | all-to-all | bytes 1703936 | tf_op jit(solution)/shard_map/all_to_all | solution.py:240
  78.2 2.3 %shard_map.62 = f32[4,104,128]{2,1,0:T(8,128)} custom-call(f32[16,104,128]{2,1,0:T(8,128)} %all_to_all.16.in_ref), custom_call_target="tpu_custom_call" | custom-call | tf_op jit(solution)/shard_map/pallas_call | solution.py:241
  80.5 11.8 %all_to_all.17.in_ref = f32[4,104,128]{2,1,0:T(8,128)} all-to-all(f32[4,104,128]{2,1,0:T(8,128)} %shard_map.62), channel_id=1, replica_groups=mesh['ctx'=32,'head'=4] {'head'}, dimensions={0} | all-to-all | bytes 425984 | tf_op jit(solution)/shard_map/all_to_all | solution.py:242
  92.3 1.8 %shard_map.63 = (bf16[6,8192]{1,0:T(8,128)(2,1)}, f32[6,64]{1,0:T(8,128)}) custom-call(f32[4,104,128]{2,1,0:T(8,128)} %all_to_all.17.in_ref), custom_call_target="tpu_custom_call" | custom-call | tf_op jit(solution)/shard_map/pallas_call | solution.py:244
Async XLA Ops:
  19.4 1.7 %copy-start = (bf16[16,96,128]{2,1,0:T(8,128)(2,1)}, bf16[16,96,128]{2,1,0:T(8,128)(2,1)S(1)}, u32[]{:S(2)}) copy-start(bf16[16,96,128]{2,1,0:T(8,128)(2,1)S(1)} %all_to_all.15.q_own) | copy-start | bytes 1179652
  19.4 1.7 %collective-permute-start = (bf16[16,96,128]{2,1,0:T(8,128)(2,1)S(1)}, bf16[16,96,128]{2,1,0:T(8,128)(2,1)S(1)}, u32[]{:S(2)}, u32[]{:S(2)}) collective-permute-start(bf16[16,96,128]{2,1,0:T(8,128)(2,1)S(1)} %all_to_all.15.q_own), channel_id=1, source_target_pairs={{0,4},{4,0},{8,12},{12,8},{16,20},{20,16},{24,28},{28,24},{32,36},... | collective-permute-start | bytes 1179656 | tf_op jit(solution)/shard_map/ppermute | solution.py:222
  21.1 0.8 copy-start.2
  51.9 2.7 %collective-permute-start.1 = (f32[2,144,768]{2,1,0:T(8,128)}, f32[2,144,768]{2,1,0:T(8,128)S(1)}, u32[]{:S(2)}, u32[]{:S(2)}) collective-permute-start(f32[2,144,768]{2,1,0:T(8,128)} %get-tuple-element.5), channel_id=1, source_target_pairs={{0,4},{4,0},{8,12},{12,8},{16,20},{20,16},{24,28},{28,24},{32,36},... | collective-permute-start | bytes 2654216 | tf_op jit(solution)/shard_map/ppermute | solution.py:238
  54.6 0.9 %copy-start.1 = (f32[2,144,768]{2,1,0:T(8,128)}, f32[2,144,768]{2,1,0:T(8,128)S(1)}, u32[]{:S(2)}) copy-start(f32[2,144,768]{2,1,0:T(8,128)S(1)} %collective-permute-done.1.b_ref) | copy-start | bytes 2654212

commit v2 on v1

v2 whole, which is shorter than its diff:
```python
import math

import jax
import jax.numpy as jnp
from jax import lax
from jax.experimental import pallas as pl
from jax.experimental.pallas import tpu as pltpu
from jax.sharding import PartitionSpec as P

DH = 128
f32, bf16 = jnp.float32, jnp.bfloat16
LOG2E = 1.4426950408889634
LN2 = 0.6931471805599453
TO_LOG2 = LOG2E / math.sqrt(DH)

CHIPS, CORES = 16, 2
TOK, GRP, KV = 6, 8, 2
ROWS = TOK * GRP
HALF = CHIPS * ROWS
COLS = CORES * HALF
CTX = 8192
CHUNKS = (1024, 3072, 4096)
STARTS = (0, 1024, 4096)
LROW, MROW, AUG = DH, DH + 8, DH + 16
RIM = 16
MSG = KV * ROWS + RIM
STEPS = 32766.0

VMEM = pl.BlockSpec(memory_space=pltpu.VMEM)
SMEM = pl.BlockSpec(memory_space=pltpu.SMEM)
ANY = pl.BlockSpec(memory_space=pl.ANY)
SMALL, LARGE = 8, 48


def spread_body(q_ref, out_ref):
    q = q_ref[...].astype(f32)
    rows = jnp.concatenate([q[:, i * DH : (i + 1) * DH] for i in range(KV * GRP)], axis=0)
    out_ref[...] = jnp.broadcast_to(rows.astype(bf16)[None], out_ref.shape)


def attend_body(
    len_ref, q_own, q_other, k_hbm, v_hbm, own_ref, other_ref, kbuf, vbuf, qt, vt, ksem, vsem
):
    outs = (own_ref, other_ref)

    def copies(c):
        part = pl.ds(STARTS[c], CHUNKS[c])
        return (
            pltpu.make_async_copy(k_hbm.at[part], kbuf.at[part], ksem.at[c]),
            pltpu.make_async_copy(v_hbm.at[part], vbuf.at[part], vsem.at[c]),
        )

    for c in range(len(CHUNKS)):
        for copy in copies(c):
            copy.start()
    valid = len_ref[0]

    def turn_queries(h):
        for i, src in enumerate((q_own, q_other)):
            x = src[:, h * ROWS : (h + 1) * ROWS, :].reshape(HALF, DH).astype(f32).T * TO_LOG2
            high = x.astype(bf16)
            qt[h, 0:DH, i * HALF : (i + 1) * HALF] = high
            qt[h, DH : 2 * DH, i * HALF : (i + 1) * HALF] = (x - high.astype(f32)).astype(bf16)

    def turn_values(h, first, size):
        ok = lax.broadcasted_iota(jnp.int32, (1, size), 1) + first < valid
        v = vbuf[pl.ds(first, size), h * DH : (h + 1) * DH].astype(f32).T
        vt[0:DH, 0:size] = jnp.where(ok, v, 0.0).astype(bf16)
        ones = jnp.broadcast_to(jnp.where(ok, 1.0, 0.0), (AUG - DH, size))
        vt[DH:AUG, 0:size] = ones.astype(bf16)

    def scores(h, i, first, size):
        k = kbuf[pl.ds(first, size), h * DH : (h + 1) * DH]
        k = jnp.concatenate([k, k], axis=1)
        return jnp.dot(k, qt[h, :, i * HALF : (i + 1) * HALF], preferred_element_type=f32)

    def chunk(c, h):
        turn_values(h, STARTS[c], CHUNKS[c])
        for i, out in enumerate(outs):
            p = jnp.exp2(scores(h, i, STARTS[c], CHUNKS[c])).astype(bf16)
            pv = jnp.dot(vt[:, 0 : CHUNKS[c]], p, preferred_element_type=f32)
            if c == 0:
                out[h] = pv
            else:
                out[h] += pv

    turn_queries(0)
    for copy in copies(0):
        copy.wait()
    chunk(0, 0)
    turn_queries(1)
    chunk(0, 1)
    for c in range(1, len(CHUNKS)):
        for copy in copies(c):
            copy.wait()

        @pl.when(STARTS[c] < valid)
        def _():
            for h in range(KV):
                chunk(c, h)

    wrong = jnp.zeros((1, HALF), f32)
    for h in range(KV):
        for out in outs:
            total = out[h, LROW : LROW + 1, :]
            fine = (total > 2.0**-60) & (total < 2.0**90)
            wrong = wrong + jnp.where(fine, 0.0, 1.0)
            out[h, MROW:AUG, :] = jnp.zeros((AUG - MROW, HALF), f32)

    @pl.when(jnp.sum(wrong) > 0.5)
    def _():
        size = 512

        def masked(h, i, first):
            pos = lax.broadcasted_iota(jnp.int32, (size, 1), 0) + first
            return jnp.where(pos < valid, scores(h, i, first, size), -1e30)

        for h in range(KV):
            for i, out in enumerate(outs):

                def top(c, best):
                    s = masked(h, i, pl.multiple_of(c * size, size))
                    return jnp.maximum(best, jnp.max(s, axis=0, keepdims=True))

                start = jnp.full((1, HALF), -1e30, f32)
                peak = lax.fori_loop(0, CTX // size, top, start)
                out[h] = jnp.zeros((AUG, HALF), f32)

                def add(c, carry):
                    first = pl.multiple_of(c * size, size)
                    turn_values(h, first, size)
                    p = jnp.exp2(masked(h, i, first) - peak).astype(bf16)
                    out[h] += jnp.dot(vt[:, 0:size], p, preferred_element_type=f32)
                    return carry

                lax.fori_loop(0, CTX // size, add, 0)
                out[h, MROW:AUG, :] = jnp.broadcast_to(peak, (AUG - MROW, HALF))


def pair_body(a_ref, b_ref, out_ref):
    for h in range(KV):
        ma, mb = a_ref[h, MROW : MROW + 1, :], b_ref[h, MROW : MROW + 1, :]
        top = jnp.maximum(ma, mb)
        wa, wb = jnp.exp2(ma - top), jnp.exp2(mb - top)
        total = wa * a_ref[h, LROW : LROW + 1, :] + wb * b_ref[h, LROW : LROW + 1, :]
        num = a_ref[h, 0:DH, :] * (wa / total) + b_ref[h, 0:DH, :] * (wb / total)
        size = jnp.max(jnp.abs(num), axis=0, keepdims=True)
        power = jnp.ceil(jnp.log2(jnp.maximum(size * 1.0001, 2.0**-100)))
        num = num * (jnp.exp2(-power) * STEPS)
        norm = (top + jnp.log2(total)) * 16.0
        coarse = jnp.floor(norm)
        fine = jnp.floor((norm - coarse) * 32767.0)
        rim = jnp.concatenate([coarse, fine, power, jnp.zeros((RIM - 3, HALF), f32)], axis=0)
        rim = rim.astype(jnp.int32)
        codes = jnp.round(num.T).astype(jnp.int32).astype(jnp.int16)
        out_ref[:, h * ROWS : (h + 1) * ROWS, :] = codes.reshape(CHIPS, ROWS, DH)
        for c in range(CHIPS):
            out_ref[c, KV * ROWS : MSG, h * ROWS : (h + 1) * ROWS] = rim[
                :, c * ROWS : (c + 1) * ROWS
            ].astype(jnp.int16)


def merge_body(in_ref, out_ref):
    rows = KV * ROWS
    rim = in_ref[:, rows:MSG, :].astype(jnp.int32).astype(f32)
    used = lax.broadcasted_iota(jnp.int32, (CHIPS, DH), 1) < rows
    norm = jnp.where(used, rim[:, 0, :] * 0.0625 + rim[:, 1, :] * (0.0625 / 32767.0), 0.0)
    power = jnp.where(used, rim[:, 2, :], 0.0)
    top = jnp.max(norm, axis=0, keepdims=True)
    w = jnp.exp2(norm - top)
    total = jnp.sum(w, axis=0, keepdims=True)
    w = (w * jnp.exp2(power) / (total * STEPS)).T
    o = jnp.zeros((rows, DH), f32)
    for c in range(CHIPS):
        o = o + in_ref[c, 0:rows, :].astype(jnp.int32).astype(f32) * w[0:rows, c : c + 1]
    parts = out_ref.shape[0]
    out_ref[:, 0:rows, :] = jnp.broadcast_to(o.astype(bf16)[None], (parts, rows, DH))
    norm = (top + jnp.log2(total)) * LN2
    pieces = []
    for _ in range(3):
        piece = norm.astype(bf16).astype(f32)
        pieces.append(piece)
        norm = norm - piece
    rim = jnp.concatenate([*pieces, jnp.zeros((RIM - 3, DH), f32)], axis=0).astype(bf16)
    out_ref[:, rows:MSG, :] = jnp.broadcast_to(rim[None], (parts, RIM, DH))


def finish_body(in_ref, mixed_ref, norm_ref):
    rows, heads = KV * ROWS, KV * GRP
    parts = in_ref.shape[0]
    token = lax.broadcasted_iota(jnp.int32, (8, DH), 0)
    lane = lax.broadcasted_iota(jnp.int32, (8, DH), 1)
    lane_of = lax.broadcasted_iota(jnp.int32, (DH, parts * heads), 0)
    head_of = lax.broadcasted_iota(jnp.int32, (DH, parts * heads), 1)
    norm = jnp.zeros((8, parts * heads), f32)
    for z in range(parts):
        o = in_ref[z, 0:rows, :].astype(f32)
        for i in range(heads):
            mixed_ref[:, (z * heads + i) * DH : (z * heads + i + 1) * DH] = o[
                i * TOK : (i + 1) * TOK, :
            ].astype(bf16)
        rim = in_ref[z, rows:MSG, :].astype(f32)
        mine = jnp.where((lane % TOK == token) & (lane < rows), rim[0:1] + rim[1:2] + rim[2:3], 0.0)
        pick = jnp.where(lane_of // TOK + z * heads == head_of, 1.0, 0.0)
        pick = jnp.where(lane_of < rows, pick, 0.0)
        norm = norm + jnp.dot(
            mine, pick, preferred_element_type=f32, precision=lax.Precision.HIGHEST
        )
    norm_ref[...] = norm[0:TOK, :]


def call(body, out_shape, in_specs, scratch=(), room=SMALL):
    many = isinstance(out_shape, tuple)
    return pl.pallas_call(
        body,
        out_shape=out_shape,
        in_specs=in_specs,
        out_specs=(VMEM,) * len(out_shape) if many else VMEM,
        scratch_shapes=list(scratch),
        compiler_params=pltpu.CompilerParams(vmem_limit_bytes=room * 2**20),
    )


def on_device(queries, keys, values, lengths):
    shape = jax.ShapeDtypeStruct
    same_core = [[2 * i + c for i in range(CHIPS)] for c in range(CORES)]
    swap = [(i, i ^ 1) for i in range(CHIPS * CORES)]
    parts = lax.axis_size("head")

    sent = call(spread_body, shape((CHIPS, KV * ROWS, DH), bf16), [VMEM])(queries)
    q_own = lax.all_to_all(sent, "ctx", 0, 0, tiled=True, axis_index_groups=same_core)
    q_other = lax.ppermute(q_own, "ctx", swap)
    acc = shape((KV, AUG, HALF), f32)
    own, other = call(
        attend_body,
        (acc, acc),
        [SMEM, VMEM, VMEM, ANY, ANY],
        [
            pltpu.VMEM((CTX, KV * DH), bf16),
            pltpu.VMEM((CTX, KV * DH), bf16),
            pltpu.VMEM((KV, 2 * DH, COLS), bf16),
            pltpu.VMEM((AUG, max(CHUNKS)), bf16),
            pltpu.SemaphoreType.DMA((len(CHUNKS),)),
            pltpu.SemaphoreType.DMA((len(CHUNKS),)),
        ],
        LARGE,
    )(lengths, q_own, q_other, keys, values)
    partner = lax.ppermute(other, "ctx", swap)
    sent = call(pair_body, shape((CHIPS, MSG, DH), jnp.int16), [VMEM, VMEM])(own, partner)
    got = lax.all_to_all(sent, "ctx", 0, 0, tiled=True, axis_index_groups=same_core)
    sent = call(merge_body, shape((parts, MSG, DH), bf16), [VMEM])(got)
    got = lax.all_to_all(sent, "head", 0, 0, tiled=True)
    heads = parts * KV * GRP
    return call(finish_body, (shape((TOK, heads * DH), bf16), shape((TOK, heads), f32)), [VMEM])(
        got
    )


def solution(mesh):
    return jax.shard_map(
        on_device,
        mesh=mesh,
        in_specs=(P("ctx", "head"), P("ctx", "head"), P("ctx", "head"), P("ctx")),
        out_specs=(P("ctx", None), P("ctx", None)),
        check_vma=False,
    )
```

time: 94.7 us -> 138 us (1.46)
  Pallas kernels: 38.4 us -> 90.2 us
  blocking collectives: 49 us -> 42 us
    pallas_call x1, Pallas kernels: 30.1 us -> 88.5 us  [on_device(): call(attend_body, (acc, acc), [SMEM, VMEM, VMEM, ANY, ANY], [pltpu.VMEM((...]
    all_to_all x2, blocking collectives: 37.1 us -> 31 us  [on_device(): lax.all_to_all(sent, 'ctx', 0, 0, tiled=True, axis_index_groups=same_core)]
    pallas_call x2, Pallas kernels: 4.98 us -> 0.84 us  [the longest x1 0.46 us: on_device(): sent = call(merge_body, shape((parts, MSG, DH), bf16), [VMEM])(got)]
    pallas_call x1, Pallas kernels: 1.53 us -> 0.03 us  [on_device(): call(spread_body, shape((CHIPS, KV * ROWS, DH), bf16), [VMEM])(queries)]
where the time goes in v2:
time: 138 us
  Pallas kernels  90.2 us (65%)
  blocking collectives  42 us (30%)
  waiting for transfers between devices  3.48 us (3%)
    pallas_call x1, Pallas kernels, on_device(): call(attend_body, (acc, acc), [SMEM, VMEM, VMEM, ANY, ANY], [pltpu.VMEM((...  88.5 us
    all_to_all x2, blocking collectives, on_device(): lax.all_to_all(sent, 'ctx', 0, 0, tiled=True, axis_index_groups=same_core)  31 us
    all_to_all x1, blocking collectives, on_device(): got = lax.all_to_all(sent, 'head', 0, 0, tiled=True)  11 us
  transfers between devices with their start and end apart: 2, of which 2 were waited for; matrix products, arithmetic and copies ran while one was open for 0% of the time, Pallas kernels for 0%

profile of v2, /device:TPU:0, one launch (start us, length us, event | category | flops | bytes accessed | tf_op | source)
XLA Modules:
  0.0 137.9 jit_solution(5481690621794206726)
XLA Ops:
  0.6 0.0 copy-start
  0.6 0.7 copy-done
  1.4 17.0 %all_to_all.15.q_own = bf16[16,96,128]{2,1,0:T(8,128)(2,1)S(1)} all-to-all(bf16[16,96,128]{2,1,0:T(8,128)(2,1)S(1)} %shard_map.59), channel_id=1, replica_groups={{0,8,16,24,32,40,48,56,64,72,80,88,96,104,112,120},{4,12,20,28,36,44,52..., dimensions={0} | all-to-all | bytes 786432 | tf_op jit(solution)/shard_map/all_to_all | solution.py:231
  18.4 0.0 collective-permute-start
  19.1 1.1 collective-permute-done.q_other
  20.1 88.5 %shard_map.60 = (f32[2,144,768]{2,1,0:T(8,128)S(1)}, f32[2,144,768]{2,1,0:T(8,128)S(1)}) custom-call(s32[1]{0:T(128)S(6)} %copy.6.len_ref, bf16[16,96,128]{2,1,0:T(8,128)(2,1)S(1)} %all_to_all.15.q_own, bf16[16,96,128]{2,1,0:T(8,128)(2,1)S(1)} %collective-permute-done.q_other, bf16[8192,256]{1,0:T(8,128)(2,1)} %k_hbm.1, bf16[8192,256]{1,0:T(8,128)(2,1)} %v_hbm.1), custom_call_target="tpu_custom_call" | custom-call | tf_op jit(solution)/shard_map/pallas_call | solution.py:234
  108.6 0.1 collective-permute-start.1
  108.7 2.4 %collective-permute-done.1.b_ref = f32[2,144,768]{2,1,0:T(8,128)S(1)} collective-permute-done((f32[2,144,768]{2,1,0:T(8,128)S(1)}, f32[2,144,768]{2,1,0:T(8,128)S(1)}, u32[]{:S(2)}, u32[]{:S(2)}) %collective-permute-start.1) | collective-permute-done | bytes 884768 | tf_op jit(solution)/shard_map/ppermute | solution.py:248
  111.1 0.4 shard_map.61
  111.5 14.0 %all_to_all.16.in_ref = s16[16,112,128]{2,1,0:T(8,128)(2,1)S(1)} all-to-all(s16[16,112,128]{2,1,0:T(8,128)(2,1)S(1)} %shard_map.61), channel_id=1, replica_groups={{0,8,16,24,32,40,48,56,64,72,80,88,96,104,112,120},{4,12,20,28,36,44,52..., dimensions={0} | all-to-all | bytes 917504 | tf_op jit(solution)/shard_map/all_to_all | solution.py:250
  125.5 0.5 shard_map.62
  126.0 11.0 %all_to_all.17.in_ref = bf16[4,112,128]{2,1,0:T(8,128)(2,1)S(1)} all-to-all(bf16[4,112,128]{2,1,0:T(8,128)(2,1)S(1)} %shard_map.62), channel_id=1, replica_groups=mesh['ctx'=32,'head'=4] {'head'}, dimensions={0} | all-to-all | bytes 229376 | tf_op jit(solution)/shard_map/all_to_all | solution.py:252
  137.0 0.9 shard_map.63
  (1 shorter events, 0.0 us)
Async XLA Ops:
  0.6 0.8 copy-start
  18.4 1.7 %collective-permute-start = (bf16[16,96,128]{2,1,0:T(8,128)(2,1)S(1)}, bf16[16,96,128]{2,1,0:T(8,128)(2,1)S(1)}, u32[]{:S(2)}, u32[]{:S(2)}) collective-permute-start(bf16[16,96,128]{2,1,0:T(8,128)(2,1)S(1)} %all_to_all.15.q_own), channel_id=1, source_target_pairs={{0,4},{4,0},{8,12},{12,8},{16,20},{20,16},{24,28},{28,24},{32,36},... | collective-permute-start | bytes 1179656 | tf_op jit(solution)/shard_map/ppermute | solution.py:232
  108.6 2.5 %collective-permute-start.1 = (f32[2,144,768]{2,1,0:T(8,128)S(1)}, f32[2,144,768]{2,1,0:T(8,128)S(1)}, u32[]{:S(2)}, u32[]{:S(2)}) collective-permute-start(f32[2,144,768]{2,1,0:T(8,128)S(1)} %get-tuple-element.5), channel_id=1, source_target_pairs={{0,4},{4,0},{8,12},{12,8},{16,20},{20,16},{24,28},{28,24},{32,36},... | collective-permute-start | bytes 2654216 | tf_op jit(solution)/shard_map/ppermute | solution.py:248

commit v3 on v2

v3 whole, which is shorter than its diff:
```python
import functools
import math

import jax
import jax.numpy as jnp
from jax import lax
from jax.experimental import pallas as pl
from jax.experimental.pallas import tpu as pltpu
from jax.sharding import PartitionSpec as P

DH = 128
f32, bf16 = jnp.float32, jnp.bfloat16
LOG2E = 1.4426950408889634
LN2 = 0.6931471805599453
TO_LOG2 = LOG2E / math.sqrt(DH)

CHIPS, CORES = 16, 2
TOK, GRP, KV = 6, 8, 2
ROWS = TOK * GRP
HALF = CHIPS * ROWS
COLS = CORES * HALF
CTX = 8192
FIRST, LATER = (1024, 3072, 4096), (4096, 4096)
LROW, MROW, AUG = DH, DH + 8, DH + 16
RIM = 16
MSG = KV * ROWS + RIM
STEPS = 32766.0

VMEM = pl.BlockSpec(memory_space=pltpu.VMEM)
SMEM = pl.BlockSpec(memory_space=pltpu.SMEM)
ANY = pl.BlockSpec(memory_space=pl.ANY)
SMALL, LARGE = 8, 40


def spread_body(q_ref, out_ref):
    q = q_ref[...].astype(f32)
    rows = jnp.concatenate([q[:, i * DH : (i + 1) * DH] for i in range(KV * GRP)], axis=0)
    out_ref[...] = jnp.broadcast_to(rows.astype(bf16)[None], out_ref.shape)


def attend_body(fresh, *refs):
    if fresh:
        len_ref, q_ref, k_hbm, v_hbm, out_ref, k_ref, vt_ref, qt, v_ref, ksem, vsem = refs
        steps = FIRST
    else:
        len_ref, q_ref, k_ref, vt_ref, out_ref, qt = refs
        steps = LATER
    valid = len_ref[0]
    starts = [sum(steps[:c]) for c in range(len(steps))]

    def copies(c):
        part = pl.ds(starts[c], steps[c])
        return (
            pltpu.make_async_copy(v_hbm.at[part], v_ref.at[part], vsem.at[c]),
            pltpu.make_async_copy(k_hbm.at[part], k_ref.at[part], ksem.at[c]),
        )

    if fresh:
        for c in range(len(steps)):
            for copy in copies(c):
                copy.start()

    def turn_values(h, c):
        part = slice(starts[c], starts[c] + steps[c])
        ok = lax.broadcasted_iota(jnp.int32, (1, steps[c]), 1) + starts[c] < valid
        v = v_ref[part, h * DH : (h + 1) * DH].T.astype(f32)
        vt_ref[h, 0:DH, part] = jnp.where(ok, v, 0.0).astype(bf16)
        ones = jnp.broadcast_to(jnp.where(ok, 1.0, 0.0), (AUG - DH, steps[c]))
        vt_ref[h, DH:AUG, part] = ones.astype(bf16)

    for h in range(KV):
        x = q_ref[:, h * ROWS : (h + 1) * ROWS, :].reshape(HALF, DH).astype(f32).T * TO_LOG2
        high = x.astype(bf16)
        qt[h, 0:DH, :] = high
        qt[h, DH : 2 * DH, :] = (x - high.astype(f32)).astype(bf16)

    def scores(h, first, size):
        k = k_ref[pl.ds(first, size), h * DH : (h + 1) * DH]
        return jnp.dot(jnp.concatenate([k, k], axis=1), qt[h], preferred_element_type=f32)

    for c in range(len(steps)):
        if fresh and c < 2:
            for later in range(c, len(steps) if c else 1):
                for copy in copies(later):
                    copy.wait()
        for h in range(KV):
            if fresh:
                turn_values(h, c)
            p = jnp.exp2(scores(h, starts[c], steps[c])).astype(bf16)
            v = vt_ref[h, :, pl.ds(starts[c], steps[c])]
            pv = jnp.dot(v, p, preferred_element_type=f32)
            if c == 0:
                out_ref[h] = pv
            else:
                out_ref[h] += pv

    wrong = jnp.zeros((1, HALF), f32)
    for h in range(KV):
        total = out_ref[h, LROW : LROW + 1, :]
        fine = (total > 2.0**-60) & (total < 2.0**90)
        wrong = wrong + jnp.where(fine, 0.0, 1.0)
        out_ref[h, MROW:AUG, :] = jnp.zeros((AUG - MROW, HALF), f32)

    @pl.when(jnp.sum(wrong) > 0.5)
    def _():
        size = 512

        def masked(h, first):
            pos = lax.broadcasted_iota(jnp.int32, (size, 1), 0) + first
            return jnp.where(pos < valid, scores(h, first, size), -1e30)

        for h in range(KV):

            def top(c, best):
                s = masked(h, pl.multiple_of(c * size, size))
                return jnp.maximum(best, jnp.max(s, axis=0, keepdims=True))

            peak = lax.fori_loop(0, CTX // size, top, jnp.full((1, HALF), -1e30, f32))
            out_ref[h] = jnp.zeros((AUG, HALF), f32)

            def add(c, carry):
                first = pl.multiple_of(c * size, size)
                p = jnp.exp2(masked(h, first) - peak).astype(bf16)
                v = vt_ref[h, :, pl.ds(first, size)]
                out_ref[h] += jnp.dot(v, p, preferred_element_type=f32)
                return carry

            lax.fori_loop(0, CTX // size, add, 0)
            out_ref[h, MROW:AUG, :] = jnp.broadcast_to(peak, (AUG - MROW, HALF))


def pair_body(a_all, b_all, out_ref):
    for h in range(KV):
        a_ref, b_ref = a_all.at[h], b_all.at[h]
        ma, mb = a_ref[MROW : MROW + 1, :], b_ref[MROW : MROW + 1, :]
        top = jnp.maximum(ma, mb)
        wa, wb = jnp.exp2(ma - top), jnp.exp2(mb - top)
        total = wa * a_ref[LROW : LROW + 1, :] + wb * b_ref[LROW : LROW + 1, :]
        num = a_ref[0:DH, :] * (wa / total) + b_ref[0:DH, :] * (wb / total)
        size = jnp.max(jnp.abs(num), axis=0, keepdims=True)
        power = jnp.ceil(jnp.log2(jnp.maximum(size * 1.0001, 2.0**-100)))
        num = num * (jnp.exp2(-power) * STEPS)
        norm = (top + jnp.log2(total)) * 16.0
        coarse = jnp.floor(norm)
        fine = jnp.floor((norm - coarse) * 32767.0)
        rim = jnp.concatenate([coarse, fine, power, jnp.zeros((RIM - 3, HALF), f32)], axis=0)
        rim = rim.astype(jnp.int32)
        codes = jnp.round(num.T).astype(jnp.int32).astype(jnp.int16)
        out_ref[:, h * ROWS : (h + 1) * ROWS, :] = codes.reshape(CHIPS, ROWS, DH)
        for c in range(CHIPS):
            out_ref[c, KV * ROWS : MSG, h * ROWS : (h + 1) * ROWS] = rim[
                :, c * ROWS : (c + 1) * ROWS
            ].astype(jnp.int16)


def merge_body(in_ref, out_ref):
    rows = KV * ROWS
    rim = in_ref[:, rows:MSG, :].astype(jnp.int32).astype(f32)
    used = lax.broadcasted_iota(jnp.int32, (CHIPS, DH), 1) < rows
    norm = jnp.where(used, rim[:, 0, :] * 0.0625 + rim[:, 1, :] * (0.0625 / 32767.0), 0.0)
    power = jnp.where(used, rim[:, 2, :], 0.0)
    top = jnp.max(norm, axis=0, keepdims=True)
    w = jnp.exp2(norm - top)
    total = jnp.sum(w, axis=0, keepdims=True)
    w = (w * jnp.exp2(power) / (total * STEPS)).T
    o = jnp.zeros((rows, DH), f32)
    for c in range(CHIPS):
        o = o + in_ref[c, 0:rows, :].astype(jnp.int32).astype(f32) * w[0:rows, c : c + 1]
    parts = out_ref.shape[0]
    out_ref[:, 0:rows, :] = jnp.broadcast_to(o.astype(bf16)[None], (parts, rows, DH))
    norm = (top + jnp.log2(total)) * LN2
    pieces = []
    for _ in range(3):
        piece = norm.astype(bf16).astype(f32)
        pieces.append(piece)
        norm = norm - piece
    rim = jnp.concatenate([*pieces, jnp.zeros((RIM - 3, DH), f32)], axis=0).astype(bf16)
    out_ref[:, rows:MSG, :] = jnp.broadcast_to(rim[None], (parts, RIM, DH))


def finish_body(in_ref, mixed_ref, norm_ref):
    rows, heads = KV * ROWS, KV * GRP
    parts = in_ref.shape[0]
    token = lax.broadcasted_iota(jnp.int32, (8, DH), 0)
    lane = lax.broadcasted_iota(jnp.int32, (8, DH), 1)
    lane_of = lax.broadcasted_iota(jnp.int32, (DH, parts * heads), 0)
    head_of = lax.broadcasted_iota(jnp.int32, (DH, parts * heads), 1)
    norm = jnp.zeros((8, parts * heads), f32)
    for z in range(parts):
        o = in_ref[z, 0:rows, :].astype(f32)
        for i in range(heads):
            mixed_ref[:, (z * heads + i) * DH : (z * heads + i + 1) * DH] = o[
                i * TOK : (i + 1) * TOK, :
            ].astype(bf16)
        rim = in_ref[z, rows:MSG, :].astype(f32)
        mine = jnp.where((lane % TOK == token) & (lane < rows), rim[0:1] + rim[1:2] + rim[2:3], 0.0)
        pick = jnp.where(lane_of // TOK + z * heads == head_of, 1.0, 0.0)
        pick = jnp.where(lane_of < rows, pick, 0.0)
        norm = norm + jnp.dot(
            mine, pick, preferred_element_type=f32, precision=lax.Precision.HIGHEST
        )
    norm_ref[...] = norm[0:TOK, :]


def call(body, out_shape, in_specs, scratch=(), room=SMALL, cost=None):
    many = isinstance(out_shape, tuple)
    return pl.pallas_call(
        body,
        out_shape=out_shape,
        in_specs=in_specs,
        out_specs=(VMEM,) * len(out_shape) if many else VMEM,
        scratch_shapes=list(scratch),
        cost_estimate=cost,
        compiler_params=pltpu.CompilerParams(vmem_limit_bytes=room * 2**20),
    )


def hbm(x):
    return pltpu.with_memory_space_constraint(x, pltpu.HBM)


def on_device(queries, keys, values, lengths):
    shape = jax.ShapeDtypeStruct
    same_core = [[2 * i + c for i in range(CHIPS)] for c in range(CORES)]
    swap = [(i, i ^ 1) for i in range(CHIPS * CORES)]
    parts = lax.axis_size("head")

    sent = call(spread_body, shape((CHIPS, KV * ROWS, DH), bf16), [VMEM])(queries)
    q_own = lax.all_to_all(sent, "ctx", 0, 0, tiled=True, axis_index_groups=same_core)
    q_other = lax.ppermute(q_own, "ctx", swap)

    def attend(fresh, *args):
        acc = shape((KV, AUG, HALF), f32)
        handed = (shape((CTX, KV * DH), bf16), shape((KV, AUG, CTX), bf16))
        scratch = [pltpu.VMEM((KV, 2 * DH, HALF), bf16)]
        if fresh:
            scratch += [pltpu.VMEM((CTX, KV * DH), bf16)]
            scratch += [pltpu.SemaphoreType.DMA((len(FIRST),))] * 2
        return call(
            functools.partial(attend_body, fresh),
            (acc, *handed) if fresh else acc,
            [SMEM, VMEM, ANY, ANY] if fresh else [SMEM, VMEM, VMEM, VMEM],
            scratch,
            LARGE,
            pl.CostEstimate(
                flops=KV * 6 * DH * HALF * CTX, bytes_accessed=2**20, transcendentals=KV * HALF * CTX
            ),
        )(*args)

    other, k, vt = attend(True, lengths, q_other, hbm(keys), hbm(values))
    partner = lax.ppermute(other, "ctx", swap)
    own = attend(False, lengths, q_own, k, vt)
    sent = call(pair_body, shape((CHIPS, MSG, DH), jnp.int16), [VMEM] * 2)(own, partner)
    got = lax.all_to_all(sent, "ctx", 0, 0, tiled=True, axis_index_groups=same_core)
    sent = call(merge_body, shape((parts, MSG, DH), bf16), [VMEM])(got)
    got = lax.all_to_all(sent, "head", 0, 0, tiled=True)
    heads = parts * KV * GRP
    return call(finish_body, (shape((TOK, heads * DH), bf16), shape((TOK, heads), f32)), [VMEM])(
        got
    )


def solution(mesh):
    return jax.shard_map(
        on_device,
        mesh=mesh,
        in_specs=(P("ctx", "head"), P("ctx", "head"), P("ctx", "head"), P("ctx")),
        out_specs=(P("ctx", None), P("ctx", None)),
        check_vma=False,
    )
```

time: 138 us -> 134 us (0.971)
  waiting for transfers between devices: 3.48 us -> 1.07 us
  blocking collectives: 42 us -> 40.4 us
    ppermute x1, waiting for transfers between devices: 2.41 us -> 0.01 us  [on_device(): partner = lax.ppermute(other, 'ctx', swap)]
    all_to_all x2, blocking collectives: 31 us -> 29.4 us  [on_device(): lax.all_to_all(sent, 'ctx', 0, 0, tiled=True, axis_index_groups=same_core)]
    pallas_call x2 -> x3, Pallas kernels: 88.8 us -> 88.6 us  [the longest x2 88.2 us: attend(): call(functools.partial(attend_body, fresh), (acc, *handed) if fresh else...]
  transfers between devices with their start and end apart: 2 -> 2, of which waited for: 2 -> 1; matrix products, arithmetic and copies ran while one was open for 0% -> 0% of each run, Pallas kernels for 0% -> 32%
where the time goes in v3:
time: 134 us
  Pallas kernels  90 us (67%)
  blocking collectives  40.4 us (30%)
  between operations  1.34 us (1%)
    pallas_call x2, Pallas kernels, attend(): call(functools.partial(attend_body, fresh), (acc, *handed) if fresh else...  88.2 us
    all_to_all x2, blocking collectives, on_device(): lax.all_to_all(sent, 'ctx', 0, 0, tiled=True, axis_index_groups=same_core)  29.4 us
    all_to_all x1, blocking collectives, on_device(): got = lax.all_to_all(sent, 'head', 0, 0, tiled=True)  11 us
  transfers between devices with their start and end apart: 2, of which 1 were waited for; matrix products, arithmetic and copies ran while one was open for 0% of the time, Pallas kernels for 32%

profile of v3, /device:TPU:0, one launch (start us, length us, event | category | flops | bytes accessed | tf_op | source)
XLA Modules:
  0.0 133.6 jit_solution(6050726773123986233)
XLA Ops:
  0.6 0.0 copy-start
  0.6 0.7 copy-done
  1.4 17.0 %all_to_all.15.refs_1_ = bf16[16,96,128]{2,1,0:T(8,128)(2,1)S(1)} all-to-all(bf16[16,96,128]{2,1,0:T(8,128)(2,1)S(1)} %shard_map.59), channel_id=1, replica_groups={{0,8,16,24,32,40,48,56,64,72,80,88,96,104,112,120},{4,12,20,28,36,44,52..., dimensions={0} | all-to-all | bytes 786432 | tf_op jit(solution)/shard_map/all_to_all | solution.py:229
  18.4 0.0 collective-permute-start
  19.1 1.1 collective-permute-done.refs_1_
  20.1 45.2 %shard_map.60 = (f32[2,144,768]{2,1,0:T(8,128)S(1)}, bf16[8192,256]{1,0:T(8,128)(2,1)S(1)}, bf16[2,144,8192]{2,1,0:T(8,128)(2,1)S(1)}) custom-call(s32[1]{0:T(128)S(6)} %copy.6.refs_0_, bf16[16,96,128]{2,1,0:T(8,128)(2,1)S(1)} %collective-permute-done.refs_1_, bf16[8192,256]{1,0:T(8,128)(2,1)} %refs_2_.1, bf16[8192,256]{1,0:T(8,128)(2,1)} %refs_3_.1), custom_call_target="tpu_custom_call" | custom-call | flops 9663676416 | bytes 1048576 | tf_op jit(solution)/shard_map/pallas_call | solution.py:239
  65.4 0.1 collective-permute-start.1
  65.5 43.0 %shard_map.61.a_all = f32[2,144,768]{2,1,0:T(8,128)S(1)} custom-call(s32[1]{0:T(128)S(6)} %copy.6.refs_0_, bf16[16,96,128]{2,1,0:T(8,128)(2,1)S(1)} %all_to_all.15.refs_1_, bf16[8192,256]{1,0:T(8,128)(2,1)S(1)} %get-tuple-element.5.refs_2_, bf16[2,144,8192]{2,1,0:T(8,128)(2,1)S(1)} %get-tuple-element.6.refs_3_), custom_call_target="tpu_custom_call" | custom-call | flops 9663676416 | bytes 1048576 | tf_op jit(solution)/shard_map/pallas_call | solution.py:239
  108.5 0.0 collective-permute-done.1.b_all
  108.5 0.4 shard_map.62
  108.9 12.4 %all_to_all.16.in_ref = s16[16,112,128]{2,1,0:T(8,128)(2,1)S(1)} all-to-all(s16[16,112,128]{2,1,0:T(8,128)(2,1)S(1)} %shard_map.62), channel_id=1, replica_groups={{0,8,16,24,32,40,48,56,64,72,80,88,96,104,112,120},{4,12,20,28,36,44,52..., dimensions={0} | all-to-all | bytes 917504 | tf_op jit(solution)/shard_map/all_to_all | solution.py:254
  121.2 0.5 shard_map.63
  121.7 11.0 %all_to_all.17.in_ref = bf16[4,112,128]{2,1,0:T(8,128)(2,1)S(1)} all-to-all(bf16[4,112,128]{2,1,0:T(8,128)(2,1)S(1)} %shard_map.63), channel_id=1, replica_groups=mesh['ctx'=32,'head'=4] {'head'}, dimensions={0} | all-to-all | bytes 229376 | tf_op jit(solution)/shard_map/all_to_all | solution.py:256
  132.7 0.9 shard_map.64
  (1 shorter events, 0.0 us)
Async XLA Ops:
  0.6 0.8 copy-start
  18.4 1.7 %collective-permute-start = (bf16[16,96,128]{2,1,0:T(8,128)(2,1)S(1)}, bf16[16,96,128]{2,1,0:T(8,128)(2,1)S(1)}, u32[]{:S(2)}, u32[]{:S(2)}) collective-permute-start(bf16[16,96,128]{2,1,0:T(8,128)(2,1)S(1)} %all_to_all.15.refs_1_), channel_id=1, source_target_pairs={{0,4},{4,0},{8,12},{12,8},{16,20},{20,16},{24,28},{28,24},{32,36},... | collective-permute-start | bytes 1179656 | tf_op jit(solution)/shard_map/ppermute | solution.py:230
  65.4 43.1 %collective-permute-start.1 = (f32[2,144,768]{2,1,0:T(8,128)S(1)}, f32[2,144,768]{2,1,0:T(8,128)S(1)}, u32[]{:S(2)}, u32[]{:S(2)}) collective-permute-start(f32[2,144,768]{2,1,0:T(8,128)S(1)} %get-tuple-element.7), channel_id=1, source_target_pairs={{0,4},{4,0},{8,12},{12,8},{16,20},{20,16},{24,28},{28,24},{32,36},... | collective-permute-start | bytes 2654216 | tf_op jit(solution)/shard_map/ppermute | solution.py:251

commit v4 on v3

--- a/solution.py
+++ b/solution.py
@@ -1,4 +1,3 @@
-import functools
 import math
 
 import jax
@@ -20,16 +19,16 @@
 HALF = CHIPS * ROWS
 COLS = CORES * HALF
 CTX = 8192
-FIRST, LATER = (1024, 3072, 4096), (4096, 4096)
+SPANS = (4096, 4096)
+TURN = 2048
 LROW, MROW, AUG = DH, DH + 8, DH + 16
 RIM = 16
 MSG = KV * ROWS + RIM
 STEPS = 32766.0
 
 VMEM = pl.BlockSpec(memory_space=pltpu.VMEM)
-SMEM = pl.BlockSpec(memory_space=pltpu.SMEM)
 ANY = pl.BlockSpec(memory_space=pl.ANY)
-SMALL, LARGE = 8, 40
+SMALL, MIDDLE, LARGE = 8, 16, 40
 
 
 def spread_body(q_ref, out_ref):
@@ -38,35 +37,21 @@
     out_ref[...] = jnp.broadcast_to(rows.astype(bf16)[None], out_ref.shape)
 
 
-def attend_body(fresh, *refs):
-    if fresh:
-        len_ref, q_ref, k_hbm, v_hbm, out_ref, k_ref, vt_ref, qt, v_ref, ksem, vsem = refs
-        steps = FIRST
-    else:
-        len_ref, q_ref, k_ref, vt_ref, out_ref, qt = refs
-        steps = LATER
-    valid = len_ref[0]
-    starts = [sum(steps[:c]) for c in range(len(steps))]
-
-    def copies(c):
-        part = pl.ds(starts[c], steps[c])
-        return (
-            pltpu.make_async_copy(v_hbm.at[part], v_ref.at[part], vsem.at[c]),
-            pltpu.make_async_copy(k_hbm.at[part], k_ref.at[part], ksem.at[c]),
-        )
-
-    if fresh:
-        for c in range(len(steps)):
-            for copy in copies(c):
-                copy.start()
-
-    def turn_values(h, c):
-        part = slice(starts[c], starts[c] + steps[c])
-        ok = lax.broadcasted_iota(jnp.int32, (1, steps[c]), 1) + starts[c] < valid
-        v = v_ref[part, h * DH : (h + 1) * DH].T.astype(f32)
-        vt_ref[h, 0:DH, part] = jnp.where(ok, v, 0.0).astype(bf16)
-        ones = jnp.broadcast_to(jnp.where(ok, 1.0, 0.0), (AUG - DH, steps[c]))
-        vt_ref[h, DH:AUG, part] = ones.astype(bf16)
+def prepare_body(len_ref, v_ref, _, vt_ref):
+    valid = len_ref[0:1, 0:1]
+    for c in range(CTX // TURN):
+        part = slice(c * TURN, (c + 1) * TURN)
+        ok = lax.broadcasted_iota(jnp.int32, (1, TURN), 1) + c * TURN < valid
+        ones = jnp.broadcast_to(jnp.where(ok, 1.0, 0.0), (AUG - DH, TURN))
+        for h in range(KV):
+            v = v_ref[part, h * DH : (h + 1) * DH].T.astype(f32)
+            vt_ref[h, 0:DH, part] = jnp.where(ok, v, 0.0).astype(bf16)
+            vt_ref[h, DH:AUG, part] = ones.astype(bf16)
+
+
+def attend_body(len_ref, q_ref, k_ref, vt_ref, out_ref, qt):
+    valid = len_ref[0:1, 0:1]
+    starts = [sum(SPANS[:c]) for c in range(len(SPANS))]
 
     for h in range(KV):
         x = q_ref[:, h * ROWS : (h + 1) * ROWS, :].reshape(HALF, DH).astype(f32).T * TO_LOG2
@@ -78,16 +63,10 @@
         k = k_ref[pl.ds(first, size), h * DH : (h + 1) * DH]
         return jnp.dot(jnp.concatenate([k, k], axis=1), qt[h], preferred_element_type=f32)
 
-    for c in range(len(steps)):
-        if fresh and c < 2:
-            for later in range(c, len(steps) if c else 1):
-                for copy in copies(later):
-                    copy.wait()
+    for c in range(len(SPANS)):
         for h in range(KV):
-            if fresh:
-                turn_values(h, c)
-            p = jnp.exp2(scores(h, starts[c], steps[c])).astype(bf16)
-            v = vt_ref[h, :, pl.ds(starts[c], steps[c])]
+            p = jnp.exp2(scores(h, starts[c], SPANS[c])).astype(bf16)
+            v = vt_ref[h, :, pl.ds(starts[c], SPANS[c])]
             pv = jnp.dot(v, p, preferred_element_type=f32)
             if c == 0:
                 out_ref[h] = pv
@@ -215,8 +194,8 @@
     )
 
 
-def hbm(x):
-    return pltpu.with_memory_space_constraint(x, pltpu.HBM)
+def vmem(x):
+    return pltpu.with_memory_space_constraint(x, pltpu.VMEM)
 
 
 def on_device(queries, keys, values, lengths):
@@ -225,31 +204,37 @@
     swap = [(i, i ^ 1) for i in range(CHIPS * CORES)]
     parts = lax.axis_size("head")
 
+    lengths = lax.ppermute(jnp.broadcast_to(lengths, (8, DH)), "ctx", swap)
+    keys, values, lengths = lax.optimization_barrier((keys, values, lengths))
+    keys, values = (vmem(lax.ppermute(x, "ctx", swap)) for x in (keys, values))
     sent = call(spread_body, shape((CHIPS, KV * ROWS, DH), bf16), [VMEM])(queries)
     q_own = lax.all_to_all(sent, "ctx", 0, 0, tiled=True, axis_index_groups=same_core)
     q_other = lax.ppermute(q_own, "ctx", swap)
 
-    def attend(fresh, *args):
-        acc = shape((KV, AUG, HALF), f32)
-        handed = (shape((CTX, KV * DH), bf16), shape((KV, AUG, CTX), bf16))
-        scratch = [pltpu.VMEM((KV, 2 * DH, HALF), bf16)]
-        if fresh:
-            scratch += [pltpu.VMEM((CTX, KV * DH), bf16)]
-            scratch += [pltpu.SemaphoreType.DMA((len(FIRST),))] * 2
+    turned = call(
+        prepare_body,
+        shape((KV, AUG, CTX), bf16),
+        [VMEM, VMEM, ANY],
+        (),
+        MIDDLE,
+        pl.CostEstimate(flops=0, bytes_accessed=9 * 2**20, transcendentals=0),
+    )(lengths, values, q_own)
+
+    def attend(q):
         return call(
-            functools.partial(attend_body, fresh),
-            (acc, *handed) if fresh else acc,
-            [SMEM, VMEM, ANY, ANY] if fresh else [SMEM, VMEM, VMEM, VMEM],
-            scratch,
+            attend_body,
+            shape((KV, AUG, HALF), f32),
+            [VMEM, VMEM, VMEM, VMEM],
+            [pltpu.VMEM((KV, 2 * DH, HALF), bf16)],
             LARGE,
             pl.CostEstimate(
                 flops=KV * 6 * DH * HALF * CTX, bytes_accessed=2**20, transcendentals=KV * HALF * CTX
             ),
-        )(*args)
-
-    other, k, vt = attend(True, lengths, q_other, hbm(keys), hbm(values))
+        )(lengths, q, keys, turned)
+
+    other = attend(q_other)
     partner = lax.ppermute(other, "ctx", swap)
-    own = attend(False, lengths, q_own, k, vt)
+    own = attend(q_own)
     sent = call(pair_body, shape((CHIPS, MSG, DH), jnp.int16), [VMEM] * 2)(own, partner)
     got = lax.all_to_all(sent, "ctx", 0, 0, tiled=True, axis_index_groups=same_core)
     sent = call(merge_body, shape((parts, MSG, DH), bf16), [VMEM])(got)

time: 134 us -> 134 us (level)
  the two profiles are of different devices: /device:TPU:0 before, /device:TPU:1 now
where the time goes in v4:
time: 134 us; the launch traced here: 133 us
  Pallas kernels  89.6 us (67%)
  blocking collectives  37 us (28%)
  starting transfers between devices  3.59 us (3%)
  between operations  1.34 us (1%)
    pallas_call x2, Pallas kernels, attend(): call(attend_body, shape((KV, AUG, HALF), f32), [VMEM, VMEM, VMEM, VMEM],...  86.7 us
    all_to_all x2, blocking collectives, on_device(): lax.all_to_all(sent, 'ctx', 0, 0, tiled=True, axis_index_groups=same_core)  27.4 us
    all_to_all x1, blocking collectives, on_device(): got = lax.all_to_all(sent, 'head', 0, 0, tiled=True)  9.56 us
  transfers between devices with their start and end apart: 5, of which 2 were waited for; matrix products, arithmetic and copies ran while one was open for 0% of the time, Pallas kernels for 33%

profile of v4, /device:TPU:1, one launch (start us, length us, event | category | flops | bytes accessed | tf_op | source)
XLA Modules:
  0.0 133.3 jit_solution(3502034396901914676)
XLA Ops:
  1.3 1.5 %collective-permute-start = (s32[8,128]{1,0:T(8,128)S(1)}, s32[8,128]{1,0:T(8,128)S(1)}, u32[]{:S(2)}, u32[]{:S(2)}) collective-permute-start(s32[8,128]{1,0:T(8,128)S(1)} %broadcast_in_dim.2), channel_id=1, source_target_pairs={{0,4},{4,0},{8,12},{12,8},{16,20},{20,16},{24,28},{28,24},{32,36},... | collective-permute-start | bytes 12296 | tf_op jit(solution)/shard_map/ppermute | solution.py:207
  2.8 0.8 collective-permute-done.len_ref
  3.6 0.3 collective-permute-start.2
  4.0 0.2 collective-permute-start.1
  4.1 0.0 copy-start
  4.1 0.8 copy-done
  4.9 16.2 %all_to_all.15._.q_ref = bf16[16,96,128]{2,1,0:T(8,128)(2,1)S(1)} all-to-all(bf16[16,96,128]{2,1,0:T(8,128)(2,1)S(1)} %shard_map.62), channel_id=1, replica_groups={{0,8,16,24,32,40,48,56,64,72,80,88,96,104,112,120},{4,12,20,28,36,44,52..., dimensions={0} | all-to-all | bytes 786432 | tf_op jit(solution)/shard_map/all_to_all | solution.py:211
  21.1 1.5 %collective-permute-start.3 = (bf16[16,96,128]{2,1,0:T(8,128)(2,1)S(1)}, bf16[16,96,128]{2,1,0:T(8,128)(2,1)S(1)}, u32[]{:S(2)}, u32[]{:S(2)}) collective-permute-start(bf16[16,96,128]{2,1,0:T(8,128)(2,1)S(1)} %all_to_all.15._.q_ref), channel_id=1, source_target_pairs={{0,4},{4,0},{8,12},{12,8},{16,20},{20,16},{24,28},{28,24},{32,36},... | collective-permute-start | bytes 1179656 | tf_op jit(solution)/shard_map/ppermute | solution.py:212
  22.6 0.0 collective-permute-done.2.v_ref
  22.6 1.1 shard_map.63.vt_ref
  23.8 0.2 collective-permute-done.3.q_ref
  23.9 0.0 collective-permute-done.1.k_ref
  23.9 43.4 %shard_map.65 = f32[2,144,768]{2,1,0:T(8,128)S(1)} custom-call(s32[8,128]{1,0:T(8,128)S(1)} %collective-permute-done.len_ref, bf16[16,96,128]{2,1,0:T(8,128)(2,1)S(1)} %collective-permute-done.3.q_ref, bf16[8192,256]{1,0:T(8,128)(2,1)S(1)} %collective-permute-done.1.k_ref, bf16[2,144,8192]{2,1,0:T(8,128)(2,1)S(1)} %shard_map.63.vt_ref), custom_call_target="tpu_custom_call" | custom-call | flops 9663676416 | bytes 1048576 | tf_op jit(solution)/shard_map/pallas_call | solution.py:224
  67.3 0.1 collective-permute-start.4
  67.4 43.4 %shard_map.64.a_all = f32[2,144,768]{2,1,0:T(8,128)S(1)} custom-call(s32[8,128]{1,0:T(8,128)S(1)} %collective-permute-done.len_ref, bf16[16,96,128]{2,1,0:T(8,128)(2,1)S(1)} %all_to_all.15._.q_ref, bf16[8192,256]{1,0:T(8,128)(2,1)S(1)} %collective-permute-done.1.k_ref, bf16[2,144,8192]{2,1,0:T(8,128)(2,1)S(1)} %shard_map.63.vt_ref), custom_call_target="tpu_custom_call" | custom-call | flops 9663676416 | bytes 1048576 | tf_op jit(solution)/shard_map/pallas_call | solution.py:224
  110.8 0.0 collective-permute-done.4.b_all
  110.8 0.4 shard_map.66
  111.2 11.2 %all_to_all.16.in_ref = s16[16,112,128]{2,1,0:T(8,128)(2,1)S(1)} all-to-all(s16[16,112,128]{2,1,0:T(8,128)(2,1)S(1)} %shard_map.66), channel_id=1, replica_groups={{0,8,16,24,32,40,48,56,64,72,80,88,96,104,112,120},{4,12,20,28,36,44,52..., dimensions={0} | all-to-all | bytes 917504 | tf_op jit(solution)/shard_map/all_to_all | solution.py:239
  122.4 0.5 shard_map.67
  122.9 9.6 %all_to_all.17.in_ref = bf16[4,112,128]{2,1,0:T(8,128)(2,1)S(1)} all-to-all(bf16[4,112,128]{2,1,0:T(8,128)(2,1)S(1)} %shard_map.67), channel_id=1, replica_groups=mesh['ctx'=32,'head'=4] {'head'}, dimensions={0} | all-to-all | bytes 229376 | tf_op jit(solution)/shard_map/all_to_all | solution.py:241
  132.4 0.9 shard_map.68
  (2 shorter events, 0.0 us)
Async XLA Ops:
  1.3 2.3 %collective-permute-start = (s32[8,128]{1,0:T(8,128)S(1)}, s32[8,128]{1,0:T(8,128)S(1)}, u32[]{:S(2)}, u32[]{:S(2)}) collective-permute-start(s32[8,128]{1,0:T(8,128)S(1)} %broadcast_in_dim.2), channel_id=1, source_target_pairs={{0,4},{4,0},{8,12},{12,8},{16,20},{20,16},{24,28},{28,24},{32,36},... | collective-permute-start | bytes 12296 | tf_op jit(solution)/shard_map/ppermute | solution.py:207
  3.6 19.0 %collective-permute-start.2 = (bf16[8192,256]{1,0:T(8,128)(2,1)}, bf16[8192,256]{1,0:T(8,128)(2,1)S(1)}, u32[]{:S(2)}, u32[]{:S(2)}) collective-permute-start(bf16[8192,256]{1,0:T(8,128)(2,1)} %param.6), channel_id=1, source_target_pairs={{0,4},{4,0},{8,12},{12,8},{16,20},{20,16},{24,28},{28,24},{32,36},... | collective-permute-start | bytes 12582920 | tf_op jit(solution)/shard_map/ppermute | solution.py:209
  4.0 20.0 %collective-permute-start.1 = (bf16[8192,256]{1,0:T(8,128)(2,1)}, bf16[8192,256]{1,0:T(8,128)(2,1)S(1)}, u32[]{:S(2)}, u32[]{:S(2)}) collective-permute-start(bf16[8192,256]{1,0:T(8,128)(2,1)} %param.5), channel_id=1, source_target_pairs={{0,4},{4,0},{8,12},{12,8},{16,20},{20,16},{24,28},{28,24},{32,36},... | collective-permute-start | bytes 12582920 | tf_op jit(solution)/shard_map/ppermute | solution.py:209
  4.1 0.8 copy-start
  21.1 2.8 %collective-permute-start.3 = (bf16[16,96,128]{2,1,0:T(8,128)(2,1)S(1)}, bf16[16,96,128]{2,1,0:T(8,128)(2,1)S(1)}, u32[]{:S(2)}, u32[]{:S(2)}) collective-permute-start(bf16[16,96,128]{2,1,0:T(8,128)(2,1)S(1)} %all_to_all.15._.q_ref), channel_id=1, source_target_pairs={{0,4},{4,0},{8,12},{12,8},{16,20},{20,16},{24,28},{28,24},{32,36},... | collective-permute-start | bytes 1179656 | tf_op jit(solution)/shard_map/ppermute | solution.py:212
  67.3 43.5 %collective-permute-start.4 = (f32[2,144,768]{2,1,0:T(8,128)S(1)}, f32[2,144,768]{2,1,0:T(8,128)S(1)}, u32[]{:S(2)}, u32[]{:S(2)}) collective-permute-start(f32[2,144,768]{2,1,0:T(8,128)S(1)} %shard_map.65), channel_id=1, source_target_pairs={{0,4},{4,0},{8,12},{12,8},{16,20},{20,16},{24,28},{28,24},{32,36},... | collective-permute-start | bytes 2654216 | tf_op jit(solution)/shard_map/ppermute | solution.py:236

commit v5 on v4

--- a/solution.py
+++ b/solution.py
@@ -20,13 +20,14 @@
 COLS = CORES * HALF
 CTX = 8192
 SPANS = (4096, 4096)
-TURN = 2048
+TURNS = (1024, 1024, 2048, 2048, 2048)
 LROW, MROW, AUG = DH, DH + 8, DH + 16
 RIM = 16
 MSG = KV * ROWS + RIM
 STEPS = 32766.0
 
 VMEM = pl.BlockSpec(memory_space=pltpu.VMEM)
+SMEM = pl.BlockSpec(memory_space=pltpu.SMEM)
 ANY = pl.BlockSpec(memory_space=pl.ANY)
 SMALL, MIDDLE, LARGE = 8, 16, 40
 
@@ -37,20 +38,32 @@
     out_ref[...] = jnp.broadcast_to(rows.astype(bf16)[None], out_ref.shape)
 
 
-def prepare_body(len_ref, v_ref, _, vt_ref):
-    valid = len_ref[0:1, 0:1]
-    for c in range(CTX // TURN):
-        part = slice(c * TURN, (c + 1) * TURN)
-        ok = lax.broadcasted_iota(jnp.int32, (1, TURN), 1) + c * TURN < valid
-        ones = jnp.broadcast_to(jnp.where(ok, 1.0, 0.0), (AUG - DH, TURN))
+def prepare_body(len_ref, k_hbm, v_hbm, _, k_ref, vt_ref, v_ref, ksem, vsem):
+    starts = [sum(TURNS[:c]) for c in range(len(TURNS))]
+
+    def values(c):
+        part = pl.ds(starts[c], TURNS[c])
+        return pltpu.make_async_copy(v_hbm.at[part], v_ref.at[part], vsem.at[c])
+
+    keys = pltpu.make_async_copy(k_hbm, k_ref, ksem)
+    for c in range(len(TURNS)):
+        values(c).start()
+    keys.start()
+    valid = len_ref[0]
+    for c in range(len(TURNS)):
+        values(c).wait()
+        part = slice(starts[c], starts[c] + TURNS[c])
+        ok = lax.broadcasted_iota(jnp.int32, (1, TURNS[c]), 1) + starts[c] < valid
+        ones = jnp.broadcast_to(jnp.where(ok, 1.0, 0.0), (AUG - DH, TURNS[c]))
         for h in range(KV):
             v = v_ref[part, h * DH : (h + 1) * DH].T.astype(f32)
             vt_ref[h, 0:DH, part] = jnp.where(ok, v, 0.0).astype(bf16)
             vt_ref[h, DH:AUG, part] = ones.astype(bf16)
+    keys.wait()
 
 
 def attend_body(len_ref, q_ref, k_ref, vt_ref, out_ref, qt):
-    valid = len_ref[0:1, 0:1]
+    valid = len_ref[0]
     starts = [sum(SPANS[:c]) for c in range(len(SPANS))]
 
     for h in range(KV):
@@ -194,8 +207,8 @@
     )
 
 
-def vmem(x):
-    return pltpu.with_memory_space_constraint(x, pltpu.VMEM)
+def hbm(x):
+    return pltpu.with_memory_space_constraint(x, pltpu.HBM)
 
 
 def on_device(queries, keys, values, lengths):
@@ -204,27 +217,28 @@
     swap = [(i, i ^ 1) for i in range(CHIPS * CORES)]
     parts = lax.axis_size("head")
 
-    lengths = lax.ppermute(jnp.broadcast_to(lengths, (8, DH)), "ctx", swap)
-    keys, values, lengths = lax.optimization_barrier((keys, values, lengths))
-    keys, values = (vmem(lax.ppermute(x, "ctx", swap)) for x in (keys, values))
-    sent = call(spread_body, shape((CHIPS, KV * ROWS, DH), bf16), [VMEM])(queries)
+    sent = call(spread_body, shape((CHIPS, KV * ROWS, DH), bf16), [VMEM])(hbm(queries))
     q_own = lax.all_to_all(sent, "ctx", 0, 0, tiled=True, axis_index_groups=same_core)
     q_other = lax.ppermute(q_own, "ctx", swap)
 
-    turned = call(
+    keys, turned = call(
         prepare_body,
-        shape((KV, AUG, CTX), bf16),
-        [VMEM, VMEM, ANY],
-        (),
+        (shape((CTX, KV * DH), bf16), shape((KV, AUG, CTX), bf16)),
+        [SMEM, ANY, ANY, ANY],
+        [
+            pltpu.VMEM((CTX, KV * DH), bf16),
+            pltpu.SemaphoreType.DMA,
+            pltpu.SemaphoreType.DMA((len(TURNS),)),
+        ],
         MIDDLE,
-        pl.CostEstimate(flops=0, bytes_accessed=9 * 2**20, transcendentals=0),
-    )(lengths, values, q_own)
+        pl.CostEstimate(flops=0, bytes_accessed=17 * 2**20, transcendentals=0),
+    )(lengths, hbm(keys), hbm(values), q_own)
 
     def attend(q):
         return call(
             attend_body,
             shape((KV, AUG, HALF), f32),
-            [VMEM, VMEM, VMEM, VMEM],
+            [SMEM, VMEM, VMEM, VMEM],
             [pltpu.VMEM((KV, 2 * DH, HALF), bf16)],
             LARGE,
             pl.CostEstimate(

time: 134 us -> 134 us (level)
  the two profiles are of different devices: /device:TPU:1 before, /device:TPU:0 now
where the time goes in v5:
time: 134 us
  Pallas kernels  91.9 us (69%)
  blocking collectives  40.4 us (30%)
  between operations  1.34 us (1%)
    pallas_call x2, Pallas kernels, attend(): call(attend_body, shape((KV, AUG, HALF), f32), [SMEM, VMEM, VMEM, VMEM],...  85.9 us
    all_to_all x2, blocking collectives, on_device(): lax.all_to_all(sent, 'ctx', 0, 0, tiled=True, axis_index_groups=same_core)  29.4 us
    all_to_all x1, blocking collectives, on_device(): got = lax.all_to_all(sent, 'head', 0, 0, tiled=True)  11 us
    pallas_call x1, Pallas kernels, on_device(): call(prepare_body, (shape((CTX, KV * DH), bf16), shape((KV, AUG, CTX), bf...  3.53 us
  transfers between devices with their start and end apart: 2, of which 0 were waited for; matrix products, arithmetic and copies ran while one was open for 0% of the time, Pallas kernels for 35%

profile of v5, /device:TPU:0, one launch (start us, length us, event | category | flops | bytes accessed | tf_op | source)
XLA Modules:
  0.0 133.7 jit_solution(11941592615318679124)
XLA Ops:
  0.6 0.8 shard_map.59
  1.4 17.0 %all_to_all.15._.q_ref = bf16[16,96,128]{2,1,0:T(8,128)(2,1)S(1)} all-to-all(bf16[16,96,128]{2,1,0:T(8,128)(2,1)S(1)} %shard_map.59), channel_id=1, replica_groups={{0,8,16,24,32,40,48,56,64,72,80,88,96,104,112,120},{4,12,20,28,36,44,52..., dimensions={0} | all-to-all | bytes 786432 | tf_op jit(solution)/shard_map/all_to_all | solution.py:221
  18.4 0.0 collective-permute-start
  19.1 3.5 %shard_map.60 = (bf16[8192,256]{1,0:T(8,128)(2,1)S(1)}, bf16[2,144,8192]{2,1,0:T(8,128)(2,1)S(1)}) custom-call(s32[1]{0:T(128)S(6)} %copy.6.len_ref, bf16[8192,256]{1,0:T(8,128)(2,1)} %k_hbm.1, bf16[8192,256]{1,0:T(8,128)(2,1)} %v_hbm.1, bf16[16,96,128]{2,1,0:T(8,128)(2,1)S(1)} %all_to_all.15._.q_ref), custom_call_target="tpu_custom_call" | custom-call | bytes 17825792 | tf_op jit(solution)/shard_map/pallas_call | solution.py:224
  22.6 0.0 collective-permute-done.q_ref
  22.6 42.9 %shard_map.62 = f32[2,144,768]{2,1,0:T(8,128)S(1)} custom-call(s32[1]{0:T(128)S(6)} %copy.6.len_ref, bf16[16,96,128]{2,1,0:T(8,128)(2,1)S(1)} %collective-permute-done.q_ref, bf16[8192,256]{1,0:T(8,128)(2,1)S(1)} %get-tuple-element.4.k_ref, bf16[2,144,8192]{2,1,0:T(8,128)(2,1)S(1)} %get-tuple-element.5.vt_ref), custom_call_target="tpu_custom_call" | custom-call | flops 9663676416 | bytes 1048576 | tf_op jit(solution)/shard_map/pallas_call | solution.py:238
  65.6 0.1 collective-permute-start.1
  65.6 43.0 %shard_map.61.a_all = f32[2,144,768]{2,1,0:T(8,128)S(1)} custom-call(s32[1]{0:T(128)S(6)} %copy.6.len_ref, bf16[16,96,128]{2,1,0:T(8,128)(2,1)S(1)} %all_to_all.15._.q_ref, bf16[8192,256]{1,0:T(8,128)(2,1)S(1)} %get-tuple-element.4.k_ref, bf16[2,144,8192]{2,1,0:T(8,128)(2,1)S(1)} %get-tuple-element.5.vt_ref), custom_call_target="tpu_custom_call" | custom-call | flops 9663676416 | bytes 1048576 | tf_op jit(solution)/shard_map/pallas_call | solution.py:238
  108.6 0.0 collective-permute-done.1.b_all
  108.6 0.4 shard_map.63
  109.0 12.4 %all_to_all.16.in_ref = s16[16,112,128]{2,1,0:T(8,128)(2,1)S(1)} all-to-all(s16[16,112,128]{2,1,0:T(8,128)(2,1)S(1)} %shard_map.63), channel_id=1, replica_groups={{0,8,16,24,32,40,48,56,64,72,80,88,96,104,112,120},{4,12,20,28,36,44,52..., dimensions={0} | all-to-all | bytes 917504 | tf_op jit(solution)/shard_map/all_to_all | solution.py:253
  121.4 0.5 shard_map.64
  121.8 11.0 %all_to_all.17.in_ref = bf16[4,112,128]{2,1,0:T(8,128)(2,1)S(1)} all-to-all(bf16[4,112,128]{2,1,0:T(8,128)(2,1)S(1)} %shard_map.64), channel_id=1, replica_groups=mesh['ctx'=32,'head'=4] {'head'}, dimensions={0} | all-to-all | bytes 229376 | tf_op jit(solution)/shard_map/all_to_all | solution.py:255
  132.8 0.9 shard_map.65
Async XLA Ops:
  18.4 4.2 %collective-permute-start = (bf16[16,96,128]{2,1,0:T(8,128)(2,1)S(1)}, bf16[16,96,128]{2,1,0:T(8,128)(2,1)S(1)}, u32[]{:S(2)}, u32[]{:S(2)}) collective-permute-start(bf16[16,96,128]{2,1,0:T(8,128)(2,1)S(1)} %all_to_all.15._.q_ref), channel_id=1, source_target_pairs={{0,4},{4,0},{8,12},{12,8},{16,20},{20,16},{24,28},{28,24},{32,36},... | collective-permute-start | bytes 1179656 | tf_op jit(solution)/shard_map/ppermute | solution.py:222
  65.6 43.1 %collective-permute-start.1 = (f32[2,144,768]{2,1,0:T(8,128)S(1)}, f32[2,144,768]{2,1,0:T(8,128)S(1)}, u32[]{:S(2)}, u32[]{:S(2)}) collective-permute-start(f32[2,144,768]{2,1,0:T(8,128)S(1)} %shard_map.62), channel_id=1, source_target_pairs={{0,4},{4,0},{8,12},{12,8},{16,20},{20,16},{24,28},{28,24},{32,36},... | collective-permute-start | bytes 2654216 | tf_op jit(solution)/shard_map/ppermute | solution.py:250
